TPU v7x, 512 devices: a whole 4x8x8 slice. The times are simulated.
512 devices in a mesh: seq: 16 (over z_lo, x), grp: 32 (over z_hi, y, core).
Axes of the slice: x: 4, y: 8, z: 8 (z_hi: 2, z_lo: 4; z = z_hi * 4 + z_lo), core: 2. Of those that a mesh axis runs over, the one named last changes fastest.
Arguments:
- compressed_vectors: bfloat16 [8192, 512], P('seq'), may hold values from -20 to 20
- starting_prototypes: float32 [8192, 512], P('grp'), may hold values from -20 to 20
- softening_scale: float32 [1], replicated, may hold values from 0.5 to 0.9
- expansion_matrix: bfloat16 [512, 32768], P(None, 'grp'), may hold values from -0.25 to 0.25
Outputs:
- decoded: bfloat16 [32, 256, 32768], P(None, 'seq', 'grp')
All inputs are finite; a program needn't handle non-finite values.
Results may differ from a plain program's by a relative error of at most 0.0075.
Values may be sent and summed in bfloat16 or wider, within the bound.
A program may use at most 64 MiB of HBM per device.

v0:
```python
import jax
import jax.numpy as jnp
from jax import lax
from jax.sharding import PartitionSpec as P

ITERS = 2


def per_device(compressed_vectors, starting_prototypes, softening_scale, expansion_matrix):
    normalizer_amount = softening_scale[0] * jnp.sqrt(jnp.float32(compressed_vectors.shape[1]))
    portion = starting_prototypes.shape[0] // lax.axis_size("seq")
    offset = lax.axis_index("seq") * portion
    centers = starting_prototypes
    own_share = lax.dynamic_slice_in_dim(starting_prototypes, offset, portion, 0)
    center_bf = centers.astype(jnp.bfloat16)
    squares = jnp.sum(centers * centers, axis=1)
    finished = None
    for iteration in range(ITERS):
        dots = lax.dot_general(
            compressed_vectors,
            center_bf,
            (((1,), (1,)), ((), ())),
            preferred_element_type=jnp.float32,
        )
        logits = (2.0 * dots - squares[None, :]) / normalizer_amount
        row_max = lax.pmax(jnp.max(logits, axis=1), "grp")
        row_total = lax.psum(jnp.sum(jnp.exp(logits - row_max[:, None]), axis=1), "grp")
        resp = (jnp.exp(logits - row_max[:, None]) / row_total[:, None]).astype(jnp.bfloat16)
        weighted = lax.dot_general(
            resp, compressed_vectors, (((0,), (0,)), ((), ())), preferred_element_type=jnp.float32
        )
        assignment_weight_total = jnp.sum(resp.astype(jnp.float32), axis=0)
        if iteration + 1 < ITERS:
            weighted, assignment_weight_total = lax.psum((weighted, assignment_weight_total), "seq")
            centers = (weighted + centers) / (assignment_weight_total[:, None] + 1.0)
            own_share = lax.dynamic_slice_in_dim(centers, offset, portion, 0)
            center_bf = centers.astype(jnp.bfloat16)
            squares = jnp.sum(centers * centers, axis=1)
        else:
            weighted, assignment_weight_total = lax.psum((weighted, assignment_weight_total), "seq")
            weighted = lax.dynamic_slice_in_dim(weighted, offset, portion, 0)
            assignment_weight_total = lax.dynamic_slice_in_dim(
                assignment_weight_total, offset, portion, 0
            )
            finished = ((weighted + own_share) / (assignment_weight_total[:, None] + 1.0)).astype(
                jnp.bfloat16
            )
    return jnp.einsum(
        "gcl,lh->gch",
        lax.all_gather(finished[None], "grp", axis=0, tiled=True),
        expansion_matrix,
        preferred_element_type=jnp.float32,
    ).astype(jnp.bfloat16)


def solution(mesh):
    placed = (P("seq", None), P("grp", None), P(), P(None, "grp"))
    return jax.shard_map(
        per_device, mesh=mesh, in_specs=placed, out_specs=P(None, "seq", "grp"), check_vma=False
    )
```

profile of v0, /device:TPU:1, one launch (start us, length us, event | category | flops | bytes accessed | tf_op | source)
XLA Modules:
  0.0 749.9 jit_solution(13231445658789149813)
XLA Ops:
  6.5 0.0 copy-start
  6.5 0.0 all-reduce.3.cloned.1.call-start
  7.3 1.2 multiply_reduce_fusion.1
  8.4 1.6 fusion.9
  10.0 0.0 copy-start.2
  10.0 90.6 %pmax.14 = f32[512]{0:T(512)S(1)} all-reduce(f32[512]{0:T(512)S(1)} %get-tuple-element.11), channel_id=1, replica_groups=mesh['seq'=16,'grp'=32] {'grp'}, use_global_device_ids=true, to_apply=%region_2.0 | all-reduce | flops 512 | bytes 4096 | tf_op jit(solution)/shard_map/pmax | solution.py:26
  100.6 0.1 fusion.5
  100.7 90.7 %psum.42 = f32[512]{0:T(512)S(1)} all-reduce(f32[512]{0:T(512)S(1)} %fusion.5), channel_id=1, replica_groups=mesh['seq'=16,'grp'=32] {'grp'}, use_global_device_ids=true, to_apply=%region_4.0 | all-reduce | flops 512 | bytes 4096 | tf_op jit(solution)/shard_map/psum | solution.py:27
  191.4 0.2 convert_reduce_fusion.1
  191.6 0.0 copy-start.1
  191.6 0.0 copy-done.2
  191.6 1.1 fusion.11
  192.7 0.0 all-reduce.3.cloned.1.call-update
  192.8 0.0 all-reduce.5.cloned.1.call-start
  192.8 36.0 %psum.44 = f32[256]{0:T(256)S(1)} all-reduce(f32[256]{0:T(256)S(1)} %get-tuple-element.9), channel_id=1, replica_groups=mesh['seq'=16,'grp'=32] {'seq'}, use_global_device_ids=true, to_apply=%region_7.0 | all-reduce | flops 256 | bytes 2048 | tf_op jit(solution)/shard_map/psum | solution.py:34
  228.8 114.6 %all-reduce.3.cloned.1.call-done = f32[256,512]{1,0:T(8,128)} async-done(((f32[256,512]{1,0:T(8,128)}), f32[256,512]{1,0:T(8,128)}) %all-reduce.3.cloned.1.call-update) | async-done | bytes 524304 | tf_op jit(solution)/shard_map/psum | solution.py:34
  343.4 0.0 copy-done.1
  343.4 1.3 multiply_reduce_fusion
  344.6 0.4 fusion.10
  345.0 94.5 %pmax.15 = f32[512]{0:T(512)S(1)} all-reduce(f32[512]{0:T(512)S(1)} %get-tuple-element.13), channel_id=1, replica_groups=mesh['seq'=16,'grp'=32] {'grp'}, use_global_device_ids=true, to_apply=%region_10.0 | all-reduce | flops 512 | bytes 4096 | tf_op jit(solution)/shard_map/pmax | solution.py:26
  439.5 0.1 fusion.6
  439.6 84.2 %psum.45 = f32[512]{0:T(512)S(1)} all-reduce(f32[512]{0:T(512)S(1)} %fusion.6), channel_id=1, replica_groups=mesh['seq'=16,'grp'=32] {'grp'}, use_global_device_ids=true, to_apply=%region_12.0 | all-reduce | flops 512 | bytes 4096 | tf_op jit(solution)/shard_map/psum | solution.py:27
  523.9 0.2 convert_reduce_fusion
  524.0 1.1 fusion.12
  525.1 0.0 all-reduce.5.cloned.1.call-update
  525.2 36.1 %psum.47 = f32[256]{0:T(256)S(1)} all-reduce(f32[256]{0:T(256)S(1)} %get-tuple-element.5), channel_id=1, replica_groups=mesh['seq'=16,'grp'=32] {'seq'}, use_global_device_ids=true, to_apply=%region_15.0 | all-reduce | flops 256 | bytes 2048 | tf_op jit(solution)/shard_map/psum | solution.py:40
  561.2 0.1 dynamic-slice_add_fusion
  561.3 114.3 %all-reduce.5.cloned.1.call-done = f32[256,512]{1,0:T(8,128)} async-done(((f32[256,512]{1,0:T(8,128)}), f32[256,512]{1,0:T(8,128)}) %all-reduce.5.cloned.1.call-update) | async-done | bytes 524304 | tf_op jit(solution)/shard_map/psum | solution.py:40
  675.6 0.8 divide_convert_fusion.2
  676.5 64.9 %all-gather = bf16[512,512]{1,0:T(8,128)(2,1)S(1)} all-gather(bf16[16,512]{1,0:T(8,128)(2,1)S(1)} %divide_convert_fusion.2), channel_id=2, replica_groups=mesh['seq'=16,'grp'=32] {'grp'}, dimensions={0}, use_global_device_ids=true | all-gather | bytes 540672 | tf_op jit(solution)/shard_map/all_gather | solution.py:50
  741.4 0.0 copy-done
  741.4 1.7 convolution_convert_fusion
  (1 shorter events, 0.0 us)
Async XLA Ops:
  6.5 734.9 %copy-start = (bf16[512,1024]{1,0:T(8,128)(2,1)S(1)}, bf16[512,1024]{1,0:T(8,128)(2,1)}, u32[]{:S(2)}) copy-start(bf16[512,1024]{1,0:T(8,128)(2,1)} %param.7) | copy-start | bytes 3145732
  6.5 336.9 %all-reduce.3.cloned.1.call-start = ((), (), s32[]{:S(2)}) async-start(), calls=%async_computation | async-start | bytes 1048576 | tf_op jit(solution)/shard_map/psum | solution.py:34
  10.0 181.6 %copy-start.2 = (bf16[512,512]{1,0:T(8,128)(2,1)S(1)}, bf16[512,512]{1,0:T(8,128)(2,1)}, u32[]{:S(2)}) copy-start(bf16[512,512]{1,0:T(8,128)(2,1)} %param.4) | copy-start | bytes 1572868
  191.6 151.8 %copy-start.1 = (f32[256,512]{1,0:T(8,128)S(1)}, f32[256,512]{1,0:T(8,128)}, u32[]{:S(2)}) copy-start(f32[256,512]{1,0:T(8,128)} %param.5) | copy-start | bytes 1572868
  192.8 482.9 %all-reduce.5.cloned.1.call-start = ((), (), s32[]{:S(2)}) async-start(), calls=%async_computation.1 | async-start | bytes 1048576 | tf_op jit(solution)/shard_map/psum | solution.py:40
Sparse Core Ops, SparseCore 0:
  192.9 150.4 all-reduce.2
  525.3 150.2 all-reduce.4
where the time goes:
time: 750 us
  blocking collectives  497 us (66%)
  waiting for transfers between devices  229 us (31%)
  between operations  14.2 us (2%)
    psum x2, waiting for transfers between devices, per_device(): lax.psum((weighted, assignment_weight_total), 'seq')  229 us
    pmax x2, blocking collectives, per_device(): row_max = lax.pmax(jnp.max(logits, axis=1), 'grp')  185 us
    psum x2, blocking collectives, per_device(): lax.psum(jnp.sum(jnp.exp(logits - row_max[:, None]), axis=1), 'grp')  175 us
    psum x2, blocking collectives, per_device(): lax.psum((weighted, assignment_weight_total), 'seq')  72 us
    all_gather x1, blocking collectives, per_device(): lax.all_gather(finished[None], 'grp', axis=0, tiled=True)  64.9 us
  transfers between devices with their start and end apart: 2, of which 2 were waited for; matrix products, arithmetic and copies ran while one was open for 0% of the time, Pallas kernels for 0%

commit v1 on v0

v1 whole, which is shorter than its diff:
```python
import functools

import jax
import jax.numpy as jnp
from jax import lax
from jax.experimental import pallas as pl
from jax.experimental.pallas import tpu as pltpu
from jax.sharding import PartitionSpec as P

MESH = pl.DeviceIdType.MESH
XS, ZL = 4, 4
ZH, YS, CORES = 2, 8, 2
ROWS = 16
F32, BF16 = jnp.float32, jnp.bfloat16


def ring(d, n):
    return min(d, n - d)


SEQ = sorted(
    [(z, x) for z in range(ZL) for x in range(XS) if z or x],
    key=lambda p: -(min(3, p[0]) + ring(p[1], XS)),
)
CHIPS = sorted(
    [(z, y) for z in range(ZH) for y in range(YS) if z or y],
    key=lambda p: -(4 * p[0] + ring(p[1], YS)),
)


def seq_index(z, x):
    me = lax.axis_index("seq")
    mz, mx = me // XS, me % XS
    pz = ((mz // 2 + z // 2) % 2) * 2 + (mz % 2 + z % 2) % 2
    return pz * XS + (mx + x) % XS


def grp_index(z, y, c):
    me = lax.axis_index("grp")
    mc, my, mz = me % CORES, (me // CORES) % YS, me // (CORES * YS)
    return (((mz + z) % ZH) * YS + (my + y) % YS) * CORES + (mc + c) % CORES


def split3(v):
    hi = v.astype(BF16)
    r = v - hi.astype(F32)
    mid = r.astype(BF16)
    lo = (r - mid.astype(F32)).astype(BF16)
    return hi.astype(F32), mid.astype(F32), lo.astype(F32)


def centre_tail(centres):
    half = -0.5 * jnp.sum(centres * centres, axis=1, keepdims=True)
    hi, mid, lo = split3(half)
    lane = lax.broadcasted_iota(jnp.int32, (centres.shape[0], 128), 1)
    tail = jnp.where(lane == 0, hi, jnp.where(lane == 1, mid, jnp.where(lane == 2, lo, 0.0)))
    return tail.astype(BF16)


def kernel(
    x_ref, c_ref, scale_ref, e_hbm, out_ref,
    xe, ce, e_ref, own, lse_buf, lse_src, w_src, w_buf, c_next, f_src, fin,
    e_sem, lse_s, lse_r, w_s, w_r, c_s, c_r, f_s, f_r, p_s, p_r,
):
    width = x_ref.shape[1]
    ext = width + 128
    seq = lax.axis_index("seq")

    barrier = pltpu.get_barrier_semaphore()
    peers = [{"seq": seq_index(z, x)} for z, x in SEQ]
    peers_chip = [{"grp": grp_index(z, y, 0)} for z, y in CHIPS]
    peers_other = [{"grp": grp_index(z, y, 1)} for z, y in CHIPS]
    partner = {"grp": grp_index(0, 0, 1)}
    everyone = [p for pair in zip(peers_chip, peers_other) for p in pair] + peers + [partner]
    for p in everyone:
        pl.semaphore_signal(barrier, inc=1, device_id=p, device_id_type=MESH)

    e_copy = pltpu.make_async_copy(e_hbm, e_ref, e_sem)
    e_copy.start()

    factor = 2.0 / (scale_ref[0] * jnp.sqrt(jnp.float32(width)))
    xe[:, :width] = x_ref[...]
    xe[:, width:] = jnp.ones((x_ref.shape[0], 128), BF16)
    c0 = c_ref[...]
    ce[:, :width] = c0.astype(BF16)
    ce[:, width:] = centre_tail(c0)

    sends = []

    def send(src, dst, ssem, rsem, device):
        copy = pltpu.make_async_remote_copy(
            src_ref=src, dst_ref=dst, send_sem=ssem, recv_sem=rsem,
            device_id=device, device_id_type=MESH,
        )
        copy.start()

    def drain(ref, sem):
        pltpu.make_async_copy(ref, ref, sem).wait()

    def iteration(i, centres):
        logits = factor * lax.dot_general(
            centres, xe[...], (((1,), (1,)), ((), ())), preferred_element_type=F32
        )
        top = jnp.max(logits, axis=0, keepdims=True)
        lse = top + jnp.log(jnp.sum(jnp.exp(logits - top), axis=0, keepdims=True))
        lse_src[i] = lse
        if i == 0:
            pl.semaphore_wait(barrier, len(everyone))
        slot = 0
        for a, b in zip(peers_chip, peers_other):
            for p in (a, b):
                send(lse_src.at[i], lse_buf.at[i, slot], lse_s.at[i], lse_r.at[i], p)
                slot += 1
        send(lse_src.at[i], lse_buf.at[i, slot], lse_s.at[i], lse_r.at[i], partner)
        drain(lse_buf.at[i], lse_r.at[i])
        others = lse_buf[i]
        m = jnp.maximum(jnp.max(others, axis=0), lse)
        total = jnp.sum(jnp.exp(others - m[None]), axis=0) + jnp.exp(lse - m)
        full = m + jnp.log(total)
        resp = jnp.exp(logits - full).astype(BF16)
        w = jnp.dot(resp, xe[...], preferred_element_type=F32)
        w_src[i, :, :width] = w[:, :width].astype(BF16)
        mass = w[:, width:]
        hi = mass.astype(BF16).astype(F32)
        lane = lax.broadcasted_iota(jnp.int32, mass.shape, 1)
        w_src[i, :, width:] = jnp.where(lane < 64, hi, mass - hi).astype(BF16)
        for k, (z, x) in enumerate(SEQ):
            rows = pl.ds(pl.multiple_of(seq_index(z, x) * ROWS, ROWS), ROWS)
            send(w_src.at[i, rows], w_buf.at[i, k], w_s.at[i], w_r.at[i], peers[k])
        mine = pl.ds(pl.multiple_of(seq * ROWS, ROWS), ROWS)
        acc = w_src[i, mine, :].astype(F32)
        drain(w_buf.at[i], w_r.at[i])
        for k in range(len(SEQ)):
            acc = acc + w_buf[i, k].astype(F32)
        total_mass = acc[:, width : width + 1] + acc[:, width + 64 : width + 65]
        return acc[:, :width], total_mass

    mine = pl.ds(pl.multiple_of(seq * ROWS, ROWS), ROWS)
    summed, mass = iteration(0, ce[...])
    centre = (summed + c_ref[mine, :]) / (mass + 1.0)
    own[...] = centre
    c_next[mine, :width] = centre.astype(BF16)
    c_next[mine, width:] = centre_tail(centre)
    for k in range(len(SEQ)):
        send(c_next.at[mine], c_next.at[mine], c_s, c_r, peers[k])
    drain(c_next.at[pl.ds(0, ROWS * len(SEQ))], c_r)

    summed, mass = iteration(1, c_next[...])
    fin[0, 0] = ((summed + own[...]) / (mass + 1.0)).astype(BF16)

    n = len(CHIPS)
    for k in range(n):
        send(fin.at[0, 0], fin.at[0, k + 1], f_s, f_r, peers_chip[k])
    drain(fin.at[0, pl.ds(1, n)], f_r)
    send(fin.at[0], fin.at[1], p_s, p_r, partner)
    e_copy.wait()
    me = lax.axis_index("grp")
    mc, my, mz = me % CORES, (me // CORES) % YS, me // (CORES * YS)

    def decode(half):
        rows = fin[half].reshape((n + 1) * ROWS, width)
        d = jnp.dot(rows, e_ref[...], preferred_element_type=F32).astype(BF16)
        for k in range(n + 1):
            z, y = (0, 0) if k == 0 else CHIPS[k - 1]
            g = (((mz + ZH - z) % ZH) * YS + (my + YS - y) % YS) * CORES + (mc + half) % CORES
            out_ref[g] = d[k * ROWS : (k + 1) * ROWS]

    decode(0)
    drain(fin.at[1], p_r)
    decode(1)

    for i in range(2):
        drain(lse_buf.at[i], lse_s.at[i])
        drain(w_buf.at[i], w_s.at[i])
    drain(c_next.at[pl.ds(0, ROWS * len(SEQ))], c_s)
    drain(fin.at[0, pl.ds(1, n)], f_s)
    drain(fin.at[1], p_s)


def solution(mesh):
    def per_device(x, c, scale, e):
        t, width = x.shape
        rows = c.shape[0]
        cols = e.shape[1]
        ext = width + 128
        n_grp = ZH * YS * CORES
        vmem = pl.BlockSpec(memory_space=pltpu.VMEM)
        dma = pltpu.SemaphoreType.DMA
        return pl.pallas_call(
            kernel,
            out_shape=jax.ShapeDtypeStruct((n_grp, ROWS, cols), BF16),
            in_specs=[
                vmem, vmem, pl.BlockSpec(memory_space=pltpu.SMEM), pl.BlockSpec(memory_space=pl.ANY),
            ],
            out_specs=vmem,
            scratch_shapes=[
                pltpu.VMEM((t, ext), BF16),
                pltpu.VMEM((rows, ext), BF16),
                pltpu.VMEM((width, cols), BF16),
                pltpu.VMEM((ROWS, width), F32),
                pltpu.VMEM((2, n_grp - 1, 1, t), F32),
                pltpu.VMEM((2, 1, t), F32),
                pltpu.VMEM((2, rows, ext), BF16),
                pltpu.VMEM((2, len(SEQ), ROWS, ext), BF16),
                pltpu.VMEM((rows, ext), BF16),
                pltpu.VMEM((ROWS, width), BF16),
                pltpu.VMEM((2, n_grp // 2, ROWS, width), BF16),
                dma, dma((2,)), dma((2,)), dma((2,)), dma((2,)), dma, dma, dma, dma, dma, dma,
            ],
            compiler_params=pltpu.CompilerParams(
                collective_id=0, has_side_effects=True, vmem_limit_bytes=40 * 2**20
            ),
            name="kmeans_decode",
        )(x, c, scale, e)

    placed = (P("seq", None), P("grp", None), P(), P(None, "grp"))
    return jax.shard_map(
        per_device, mesh=mesh, in_specs=placed, out_specs=P(None, "seq", "grp"), check_vma=False
    )
```

time: 750 us -> 74.3 us (0.10)
  blocking collectives: 497 us -> 0 us
  waiting for transfers between devices: 229 us -> 0 us
  Pallas kernels: 0 us -> 69.1 us
  between operations: 14.2 us -> 0.67 us
    psum x4 -> x0, blocking collectives: 247 us -> none  [the longest x2 175 us: per_device(): lax.psum(jnp.sum(jnp.exp(logits - row_max[:, None]), axis=1), 'grp')]
    psum x2 -> x0, waiting for transfers between devices: 229 us -> none  [per_device(): lax.psum((weighted, assignment_weight_total), 'seq')]
    pmax x2 -> x0, blocking collectives: 185 us -> none  [per_device(): row_max = lax.pmax(jnp.max(logits, axis=1), 'grp')]
    pallas_call x0 -> x1, Pallas kernels: none -> 69.1 us  [per_device(): pl.pallas_call(kernel, out_shape=jax.ShapeDtypeStruct((n_grp, ROWS, cols)...]
    all_gather x1 -> x0, blocking collectives: 64.9 us -> none  [per_device(): lax.all_gather(finished[None], 'grp', axis=0, tiled=True)]
  transfers between devices with their start and end apart: 2 -> 0, of which waited for: 2 -> 0; matrix products, arithmetic and copies ran while one was open for 0% -> 0% of each run, Pallas kernels for 0% -> 0%
where the time goes in v1:
time: 74.3 us; the launch traced here: 74 us
  Pallas kernels  69.1 us (93%)
  local copies, waits for them, and re-layouts  4.27 us (6%)
    pallas_call x1, Pallas kernels, per_device(): pl.pallas_call(kernel, out_shape=jax.ShapeDtypeStruct((n_grp, ROWS, cols)...  69.1 us
    unnamed x7, local copies, waits for them, and re-layouts  4.27 us

profile of v1, /device:TPU:1, one launch (start us, length us, event | category | flops | bytes accessed | tf_op | source)
XLA Modules:
  0.0 74.0 jit_solution(12252253243681167569)
XLA Ops:
  0.7 0.0 copy-start
  0.7 1.2 %copy-done = bf16[512,1024]{1,0:T(8,128)(2,1)S(1)} copy-done((bf16[512,1024]{1,0:T(8,128)(2,1)S(1)}, bf16[512,1024]{1,0:T(8,128)(2,1)}, u32[]{:S(2)}) %copy-start) | copy-done | bytes 1048600
  1.9 0.0 copy-start.1
  1.9 1.0 %copy-done.1 = bf16[512,512]{1,0:T(8,128)(2,1)S(1)} copy-done((bf16[512,512]{1,0:T(8,128)(2,1)S(1)}, bf16[512,512]{1,0:T(8,128)(2,1)}, u32[]{:S(2)}) %copy-start.1) | copy-done | bytes 524312
  2.9 0.0 copy-start.2
  2.9 1.0 %copy-done.2 = f32[256,512]{1,0:T(8,128)S(1)} copy-done((f32[256,512]{1,0:T(8,128)S(1)}, f32[256,512]{1,0:T(8,128)}, u32[]{:S(2)}) %copy-start.2) | copy-done | bytes 524312
  4.0 69.1 %kmeans_decode.1 = bf16[32,16,1024]{2,1,0:T(8,128)(2,1)S(1)} custom-call(bf16[512,512]{1,0:T(8,128)(2,1)S(1)} %copy-done.1, f32[256,512]{1,0:T(8,128)S(1)} %copy-done.2, f32[1]{0:T(128)S(6)} %copy.6.scale_ref, bf16[512,1024]{1,0:T(8,128)(2,1)S(1)} %copy-done), custom_call_target="tpu_custom_call" | custom-call | tf_op jit(solution)/shard_map/kmeans_decode/pallas_call | solution.py:189
  73.1 1.0 %copy.7 = bf16[32,16,1024]{2,1,0:T(8,128)(2,1)} copy(bf16[32,16,1024]{2,1,0:T(8,128)(2,1)S(1)} %kmeans_decode.1) | data formatting | bytes 2097152
Async XLA Ops:
  0.7 1.2 %copy-start = (bf16[512,1024]{1,0:T(8,128)(2,1)S(1)}, bf16[512,1024]{1,0:T(8,128)(2,1)}, u32[]{:S(2)}) copy-start(bf16[512,1024]{1,0:T(8,128)(2,1)} %e_hbm.1) | copy-start | bytes 3145732
  1.9 1.0 %copy-start.1 = (bf16[512,512]{1,0:T(8,128)(2,1)S(1)}, bf16[512,512]{1,0:T(8,128)(2,1)}, u32[]{:S(2)}) copy-start(bf16[512,512]{1,0:T(8,128)(2,1)} %x_ref.1) | copy-start | bytes 1572868
  2.9 1.0 %copy-start.2 = (f32[256,512]{1,0:T(8,128)S(1)}, f32[256,512]{1,0:T(8,128)}, u32[]{:S(2)}) copy-start(f32[256,512]{1,0:T(8,128)} %c_ref.1) | copy-start | bytes 1572868

commit v2 on v1

--- a/solution.py
+++ b/solution.py
@@ -58,13 +58,16 @@
 
 
 def kernel(
-    x_ref, c_ref, scale_ref, e_hbm, out_ref,
-    xe, ce, e_ref, own, lse_buf, lse_src, w_src, w_buf, c_next, f_src, fin,
-    e_sem, lse_s, lse_r, w_s, w_r, c_s, c_r, f_s, f_r, p_s, p_r,
+    x_hbm, c_hbm, scale_ref, e_hbm, out_ref,
+    xe, c_ref, ce, e_ref, own, lse_buf, lse_src, w_src, w_buf, c_next, fin,
+    x_sem, c_sem, e_sem, lse_s, lse_r, w_s, w_r, c_s, c_r, f_s, f_r, p_s, p_r,
 ):
-    width = x_ref.shape[1]
-    ext = width + 128
+    tokens, width = x_hbm.shape
     seq = lax.axis_index("seq")
+    c_copy = pltpu.make_async_copy(c_hbm, c_ref, c_sem)
+    c_copy.start()
+    x_copy = pltpu.make_async_copy(x_hbm, xe.at[:, pl.ds(0, width)], x_sem)
+    x_copy.start()
 
     barrier = pltpu.get_barrier_semaphore()
     peers = [{"seq": seq_index(z, x)} for z, x in SEQ]
@@ -79,13 +82,14 @@
     e_copy.start()
 
     factor = 2.0 / (scale_ref[0] * jnp.sqrt(jnp.float32(width)))
-    xe[:, :width] = x_ref[...]
-    xe[:, width:] = jnp.ones((x_ref.shape[0], 128), BF16)
+    xe[:, width:] = jnp.ones((tokens, 128), BF16)
+    c_copy.wait()
     c0 = c_ref[...]
     ce[:, :width] = c0.astype(BF16)
     ce[:, width:] = centre_tail(c0)
 
-    sends = []
+    x_copy.wait()
+    pending = [e_copy.wait]
 
     def send(src, dst, ssem, rsem, device):
         copy = pltpu.make_async_remote_copy(
@@ -112,6 +116,7 @@
                 send(lse_src.at[i], lse_buf.at[i, slot], lse_s.at[i], lse_r.at[i], p)
                 slot += 1
         send(lse_src.at[i], lse_buf.at[i, slot], lse_s.at[i], lse_r.at[i], partner)
+        pending.append(lambda: drain(lse_buf.at[i], lse_s.at[i]))
         drain(lse_buf.at[i], lse_r.at[i])
         others = lse_buf[i]
         m = jnp.maximum(jnp.max(others, axis=0), lse)
@@ -127,7 +132,7 @@
         for k, (z, x) in enumerate(SEQ):
             rows = pl.ds(pl.multiple_of(seq_index(z, x) * ROWS, ROWS), ROWS)
             send(w_src.at[i, rows], w_buf.at[i, k], w_s.at[i], w_r.at[i], peers[k])
-        mine = pl.ds(pl.multiple_of(seq * ROWS, ROWS), ROWS)
+        pending.append(lambda: drain(w_buf.at[i], w_s.at[i]))
         acc = w_src[i, mine, :].astype(F32)
         drain(w_buf.at[i], w_r.at[i])
         for k in range(len(SEQ)):
@@ -143,7 +148,9 @@
     c_next[mine, width:] = centre_tail(centre)
     for k in range(len(SEQ)):
         send(c_next.at[mine], c_next.at[mine], c_s, c_r, peers[k])
-    drain(c_next.at[pl.ds(0, ROWS * len(SEQ))], c_r)
+    rest = c_next.at[pl.ds(0, ROWS * len(SEQ))]
+    pending.append(lambda: drain(rest, c_s))
+    drain(rest, c_r)
 
     summed, mass = iteration(1, c_next[...])
     fin[0, 0] = ((summed + own[...]) / (mass + 1.0)).astype(BF16)
@@ -151,9 +158,11 @@
     n = len(CHIPS)
     for k in range(n):
         send(fin.at[0, 0], fin.at[0, k + 1], f_s, f_r, peers_chip[k])
+    pending.append(lambda: drain(fin.at[0, pl.ds(1, n)], f_s))
     drain(fin.at[0, pl.ds(1, n)], f_r)
     send(fin.at[0], fin.at[1], p_s, p_r, partner)
-    e_copy.wait()
+    pending.append(lambda: drain(fin.at[1], p_s))
+    pending.pop(0)()
     me = lax.axis_index("grp")
     mc, my, mz = me % CORES, (me // CORES) % YS, me // (CORES * YS)
 
@@ -169,12 +178,8 @@
     drain(fin.at[1], p_r)
     decode(1)
 
-    for i in range(2):
-        drain(lse_buf.at[i], lse_s.at[i])
-        drain(w_buf.at[i], w_s.at[i])
-    drain(c_next.at[pl.ds(0, ROWS * len(SEQ))], c_s)
-    drain(fin.at[0, pl.ds(1, n)], f_s)
-    drain(fin.at[1], p_s)
+    for wait in pending:
+        wait()
 
 
 def solution(mesh):
@@ -185,16 +190,18 @@
         ext = width + 128
         n_grp = ZH * YS * CORES
         vmem = pl.BlockSpec(memory_space=pltpu.VMEM)
+        hbm = pl.BlockSpec(memory_space=pl.ANY)
         dma = pltpu.SemaphoreType.DMA
         return pl.pallas_call(
             kernel,
             out_shape=jax.ShapeDtypeStruct((n_grp, ROWS, cols), BF16),
             in_specs=[
-                vmem, vmem, pl.BlockSpec(memory_space=pltpu.SMEM), pl.BlockSpec(memory_space=pl.ANY),
+                hbm, hbm, pl.BlockSpec(memory_space=pltpu.SMEM), hbm,
             ],
             out_specs=vmem,
             scratch_shapes=[
                 pltpu.VMEM((t, ext), BF16),
+                pltpu.VMEM((rows, width), F32),
                 pltpu.VMEM((rows, ext), BF16),
                 pltpu.VMEM((width, cols), BF16),
                 pltpu.VMEM((ROWS, width), F32),
@@ -203,12 +210,11 @@
                 pltpu.VMEM((2, rows, ext), BF16),
                 pltpu.VMEM((2, len(SEQ), ROWS, ext), BF16),
                 pltpu.VMEM((rows, ext), BF16),
-                pltpu.VMEM((ROWS, width), BF16),
                 pltpu.VMEM((2, n_grp // 2, ROWS, width), BF16),
-                dma, dma((2,)), dma((2,)), dma((2,)), dma((2,)), dma, dma, dma, dma, dma, dma,
+                dma, dma, dma, dma((2,)), dma((2,)), dma((2,)), dma((2,)), dma, dma, dma, dma, dma, dma,
             ],
             compiler_params=pltpu.CompilerParams(
-                collective_id=0, has_side_effects=True, vmem_limit_bytes=40 * 2**20
+                collective_id=0, has_side_effects=True, vmem_limit_bytes=56 * 2**20
             ),
             name="kmeans_decode",
         )(x, c, scale, e)

time: 74.3 us -> 73.2 us (0.985)
  local copies, waits for them, and re-layouts: 4.27 us -> 2.31 us
  Pallas kernels: 69.1 us -> 70.1 us
    unnamed x7 -> x1, local copies, waits for them, and re-layouts: 4.27 us -> 2.31 us
    pallas_call x1, Pallas kernels: 69.1 us -> 70.1 us  [per_device(): pl.pallas_call(kernel, out_shape=jax.ShapeDtypeStruct((n_grp, ROWS, cols)...]
where the time goes in v2:
time: 73.2 us; the launch traced here: 73.1 us
  Pallas kernels  70.1 us (96%)
  local copies, waits for them, and re-layouts  2.31 us (3%)
    pallas_call x1, Pallas kernels, per_device(): pl.pallas_call(kernel, out_shape=jax.ShapeDtypeStruct((n_grp, ROWS, cols)...  70.1 us
    unnamed x1, local copies, waits for them, and re-layouts  2.31 us

profile of v2, /device:TPU:1, one launch (start us, length us, event | category | flops | bytes accessed | tf_op | source)
XLA Modules:
  0.0 73.1 jit_solution(10637430606358119738)
XLA Ops:
  0.7 70.1 %kmeans_decode.1 = bf16[32,16,1024]{2,1,0:T(8,128)(2,1)} custom-call(bf16[512,512]{1,0:T(8,128)(2,1)} %x_hbm.1, f32[256,512]{1,0:T(8,128)} %c_hbm.1, f32[1]{0:T(128)S(6)} %copy.6.scale_ref, bf16[512,1024]{1,0:T(8,128)(2,1)} %e_hbm.1), custom_call_target="tpu_custom_call" | custom-call | tf_op jit(solution)/shard_map/kmeans_decode/pallas_call | solution.py:195
  70.8 2.3 %copy.7 = bf16[32,16,1024]{2,1,0:T(8,128)(2,1)} copy(bf16[32,16,1024]{2,1,0:T(8,128)(2,1)} %kmeans_decode.1) | data formatting | bytes 2097152

commit v3 on v2

v3 whole, which is shorter than its diff:
```python
import functools

import jax
import jax.numpy as jnp
from jax import lax
from jax.experimental import pallas as pl
from jax.experimental.pallas import tpu as pltpu
from jax.sharding import PartitionSpec as P

MESH = pl.DeviceIdType.MESH
XS, ZL = 4, 4
ZH, YS, CORES = 2, 8, 2
ROWS = 16
F32, BF16 = jnp.float32, jnp.bfloat16


def ring(d, n):
    return min(d, n - d)


SEQ = sorted(
    [(z, x) for z in range(ZL) for x in range(XS) if z or x],
    key=lambda p: -(min(3, p[0]) + ring(p[1], XS)),
)
NEAR = sorted([(0, y) for y in range(1, YS)], key=lambda p: -ring(p[1], YS))
FAR = sorted([(1, y) for y in range(YS)], key=lambda p: -ring(p[1], YS))
CHIPS = FAR + NEAR


def seq_index(z, x):
    me = lax.axis_index("seq")
    mz, mx = me // XS, me % XS
    pz = ((mz // 2 + z // 2) % 2) * 2 + (mz % 2 + z % 2) % 2
    return pz * XS + (mx + x) % XS


def grp_index(z, y, c):
    me = lax.axis_index("grp")
    mc, my, mz = me % CORES, (me // CORES) % YS, me // (CORES * YS)
    return (((mz + z) % ZH) * YS + (my + y) % YS) * CORES + (mc + c) % CORES


def kernel(
    x_hbm, c_hbm, scale_ref, e_hbm, out_ref,
    x_ref, c_ref, e_ref, own, lse_buf, lse_src, mass_buf, mass_src,
    w_src, w_buf, c_next, sq_buf, fin,
    x_sem, c_sem, e_sem,
    lse_s, lse_r, m_s, m_r, w_s, w_r, c_s, c_r, q_s, q_r, f_s, f_r, p_s, p_r,
):
    tokens, width = x_hbm.shape
    rows = c_hbm.shape[0]
    seq = lax.axis_index("seq")
    peers = [{"seq": seq_index(z, x)} for z, x in SEQ]
    peers_chip = [{"grp": grp_index(z, y, 0)} for z, y in CHIPS]
    peers_other = [{"grp": grp_index(z, y, 1)} for z, y in CHIPS]
    partner = {"grp": grp_index(0, 0, 1)}
    everyone = [p for pair in zip(peers_chip, peers_other) for p in pair] + peers + [partner]

    c_copy = pltpu.make_async_copy(c_hbm, c_ref, c_sem)
    c_copy.start()
    x_copy = pltpu.make_async_copy(x_hbm, x_ref, x_sem)
    x_copy.start()
    barrier = pltpu.get_barrier_semaphore()
    for p in everyone:
        pl.semaphore_signal(barrier, inc=1, device_id=p, device_id_type=MESH)
    e_copy = pltpu.make_async_copy(e_hbm, e_ref, e_sem)
    e_copy.start()
    pending = [e_copy.wait]

    def send(src, dst, ssem, rsem, device):
        pltpu.make_async_remote_copy(
            src_ref=src, dst_ref=dst, send_sem=ssem, recv_sem=rsem,
            device_id=device, device_id_type=MESH,
        ).start()

    def drain(ref, sem):
        pltpu.make_async_copy(ref, ref, sem).wait()

    c_copy.wait()
    c0 = c_ref[...]
    c0_bf = c0.astype(BF16)
    half0 = 0.5 * jnp.sum(c0 * c0, axis=1, keepdims=True)
    factor = 2.0 / (scale_ref[0] * jnp.sqrt(jnp.float32(width)))
    x_copy.wait()
    mine = pl.ds(pl.multiple_of(seq * ROWS, ROWS), ROWS)
    place = lax.broadcasted_iota(jnp.int32, (ROWS, rows), 1) == (
        seq * ROWS + lax.broadcasted_iota(jnp.int32, (ROWS, rows), 0)
    )

    def iteration(i, centres, half):
        dots = lax.dot_general(
            centres, x_ref[...], (((1,), (1,)), ((), ())), preferred_element_type=F32
        )
        logits = factor * (dots - half)
        top = jnp.max(logits, axis=0, keepdims=True)
        lse = top + jnp.log(jnp.sum(jnp.exp(logits - top), axis=0, keepdims=True))
        lse_src[i] = lse
        if i == 0:
            pl.semaphore_wait(barrier, len(everyone))
        slot = 0
        for a, b in zip(peers_chip, peers_other):
            for p in (a, b):
                send(lse_src.at[i], lse_buf.at[i, slot], lse_s.at[i], lse_r.at[i], p)
                slot += 1
        send(lse_src.at[i], lse_buf.at[i, slot], lse_s.at[i], lse_r.at[i], partner)
        pending.append(lambda: drain(lse_buf.at[i], lse_s.at[i]))
        drain(lse_buf.at[i], lse_r.at[i])
        others = lse_buf[i]
        m = jnp.maximum(jnp.max(others, axis=0), lse)
        total = jnp.sum(jnp.exp(others - m[None]), axis=0) + jnp.exp(lse - m)
        full = m + jnp.log(total)
        resp = jnp.exp(logits - full).astype(BF16)
        mass = lax.dot_general(
            jnp.ones((16, tokens), BF16), resp, (((1,), (1,)), ((), ())), preferred_element_type=F32
        )[0:1]
        mass_src[i] = mass
        for k in range(len(SEQ)):
            send(mass_src.at[i], mass_buf.at[i, k], m_s.at[i], m_r.at[i], peers[k])
        w = jnp.dot(resp, x_ref[...], preferred_element_type=F32)
        w_src[i] = w.astype(BF16)
        for k, (z, x) in enumerate(SEQ):
            theirs = pl.ds(pl.multiple_of(seq_index(z, x) * ROWS, ROWS), ROWS)
            send(w_src.at[i, theirs], w_buf.at[i, k], w_s.at[i], w_r.at[i], peers[k])
        pending.append(lambda: drain(mass_buf.at[i], m_s.at[i]))
        pending.append(lambda: drain(w_buf.at[i], w_s.at[i]))
        acc = w_src[i, mine, :].astype(F32)
        drain(mass_buf.at[i], m_r.at[i])
        mass = mass + jnp.sum(mass_buf[i], axis=0)
        column = jnp.sum(jnp.where(place, mass, 0.0), axis=1, keepdims=True)
        drain(w_buf.at[i], w_r.at[i])
        for k in range(len(SEQ)):
            acc = acc + w_buf[i, k].astype(F32)
        return acc, column

    summed, column = iteration(0, c0_bf, half0)
    centre = (summed + c_ref[mine, :]) / (column + 1.0)
    own[...] = centre
    c_next[mine, :] = centre.astype(BF16)
    for k in range(len(SEQ)):
        send(c_next.at[mine], c_next.at[mine], c_s, c_r, peers[k])
    half = 0.5 * jnp.sum(centre * centre, axis=1, keepdims=True)
    sq_buf[seq] = jnp.sum(jnp.where(place, half, 0.0), axis=0, keepdims=True)
    for k in range(len(SEQ)):
        send(sq_buf.at[seq], sq_buf.at[seq], q_s, q_r, peers[k])
    n_seq = len(SEQ)
    blocks = c_next.at[pl.ds(0, ROWS * n_seq)]
    lines = sq_buf.at[pl.ds(0, n_seq)]
    pending.append(lambda: drain(blocks, c_s))
    pending.append(lambda: drain(lines, q_s))
    drain(lines, q_r)
    line = jnp.sum(sq_buf[...], axis=0)
    diagonal = lax.broadcasted_iota(jnp.int32, (rows, rows), 0) == lax.broadcasted_iota(
        jnp.int32, (rows, rows), 1
    )
    half1 = jnp.sum(jnp.where(diagonal, line, 0.0), axis=1, keepdims=True)
    drain(blocks, c_r)

    summed, column = iteration(1, c_next[...], half1)
    fin[0, 0] = ((summed + own[...]) / (column + 1.0)).astype(BF16)

    near, far = len(NEAR), len(FAR)
    slots = [1 + near + k for k in range(far)] + [1 + k for k in range(near)]
    for k, slot in enumerate(slots):
        g = 1 if k < far else 0
        send(fin.at[0, 0], fin.at[0, slot], f_s.at[g], f_r.at[g], peers_chip[k])
    parts = (fin.at[0, pl.ds(1, near)], fin.at[0, pl.ds(1 + near, far)])
    halves = [[fin.at[c, pl.ds(g * (1 + near), far)] for g in range(2)] for c in range(2)]
    for g in range(2):
        pending.append(lambda g=g: drain(parts[g], f_s.at[g]))
    drain(parts[0], f_r.at[0])
    send(halves[0][0], halves[1][0], p_s.at[0], p_r.at[0], partner)
    pending.append(lambda: drain(halves[1][0], p_s.at[0]))
    drain(parts[1], f_r.at[1])
    send(halves[0][1], halves[1][1], p_s.at[1], p_r.at[1], partner)
    pending.append(lambda: drain(halves[1][1], p_s.at[1]))
    pending.pop(0)()
    me = lax.axis_index("grp")
    mc, my, mz = me % CORES, (me // CORES) % YS, me // (CORES * YS)
    chips = [(0, 0)] + NEAR + FAR

    def decode(half, first, count):
        part = fin[half, first : first + count].reshape(count * ROWS, width)
        d = jnp.dot(part, e_ref[...], preferred_element_type=F32).astype(BF16)
        for k in range(count):
            z, y = chips[first + k]
            g = (((mz + ZH - z) % ZH) * YS + (my + YS - y) % YS) * CORES + (mc + half) % CORES
            out_ref[g] = d[k * ROWS : (k + 1) * ROWS]

    decode(0, 0, 2 * far)
    drain(halves[1][0], p_r.at[0])
    decode(1, 0, far)
    drain(halves[1][1], p_r.at[1])
    decode(1, far, far)

    for wait in pending:
        wait()


def solution(mesh):
    def per_device(x, c, scale, e):
        t, width = x.shape
        rows = c.shape[0]
        cols = e.shape[1]
        n_grp = ZH * YS * CORES
        n_seq = XS * ZL
        hbm = pl.BlockSpec(memory_space=pltpu.HBM)
        dma = pltpu.SemaphoreType.DMA
        x, c, e = (pltpu.with_memory_space_constraint(v, pltpu.HBM) for v in (x, c, e))
        return pl.pallas_call(
            kernel,
            out_shape=jax.ShapeDtypeStruct((n_grp, ROWS, cols), BF16),
            in_specs=[hbm, hbm, pl.BlockSpec(memory_space=pltpu.SMEM), hbm],
            out_specs=pl.BlockSpec(memory_space=pltpu.VMEM),
            scratch_shapes=[
                pltpu.VMEM((t, width), BF16),
                pltpu.VMEM((rows, width), F32),
                pltpu.VMEM((width, cols), BF16),
                pltpu.VMEM((ROWS, width), F32),
                pltpu.VMEM((2, n_grp - 1, 1, t), F32),
                pltpu.VMEM((2, 1, t), F32),
                pltpu.VMEM((2, n_seq - 1, 1, rows), F32),
                pltpu.VMEM((2, 1, rows), F32),
                pltpu.VMEM((2, rows, width), BF16),
                pltpu.VMEM((2, n_seq - 1, ROWS, width), BF16),
                pltpu.VMEM((rows, width), BF16),
                pltpu.VMEM((n_seq, 1, rows), F32),
                pltpu.VMEM((2, n_grp // 2, ROWS, width), BF16),
                dma, dma, dma,
                dma((2,)), dma((2,)), dma((2,)), dma((2,)), dma((2,)), dma((2,)),
                dma, dma, dma, dma,
                dma((2,)), dma((2,)), dma((2,)), dma((2,)),
            ],
            compiler_params=pltpu.CompilerParams(
                collective_id=0, has_side_effects=True, vmem_limit_bytes=24 * 2**20
            ),
            name="kmeans_decode",
        )(x, c, scale, e)

    placed = (P("seq", None), P("grp", None), P(), P(None, "grp"))
    return jax.shard_map(
        per_device, mesh=mesh, in_specs=placed, out_specs=P(None, "seq", "grp"), check_vma=False
    )
```

time: 73.2 us -> 69.5 us (0.949)
  Pallas kernels: 70.1 us -> 67.7 us
  local copies, waits for them, and re-layouts: 2.31 us -> 0.97 us
    pallas_call x1, Pallas kernels: 70.1 us -> 67.7 us  [per_device(): pl.pallas_call(kernel, out_shape=jax.ShapeDtypeStruct((n_grp, ROWS, cols)...]
    unnamed x1, local copies, waits for them, and re-layouts: 2.31 us -> 0.97 us
where the time goes in v3:
time: 69.5 us; the launch traced here: 69.4 us
  Pallas kernels  67.7 us (97%)
  local copies, waits for them, and re-layouts  0.97 us (1%)
    pallas_call x1, Pallas kernels, per_device(): pl.pallas_call(kernel, out_shape=jax.ShapeDtypeStruct((n_grp, ROWS, cols)...  67.7 us

profile of v3, /device:TPU:1, one launch (start us, length us, event | category | flops | bytes accessed | tf_op | source)
XLA Modules:
  0.0 69.4 jit_solution(4958395053631499086)
XLA Ops:
  0.7 67.7 %kmeans_decode.1 = bf16[32,16,1024]{2,1,0:T(8,128)(2,1)S(1)} custom-call(bf16[512,512]{1,0:T(8,128)(2,1)} %x_hbm.1, f32[256,512]{1,0:T(8,128)} %c_hbm.1, f32[1]{0:T(128)S(6)} %copy.6.scale_ref, bf16[512,1024]{1,0:T(8,128)(2,1)} %e_hbm.1), custom_call_target="tpu_custom_call" | custom-call | tf_op jit(solution)/shard_map/kmeans_decode/pallas_call | solution.py:209
  68.4 1.0 %copy.7 = bf16[32,16,1024]{2,1,0:T(8,128)(2,1)} copy(bf16[32,16,1024]{2,1,0:T(8,128)(2,1)S(1)} %kmeans_decode.1) | data formatting | bytes 2097152

commit v4 on v3

--- a/solution.py
+++ b/solution.py
@@ -78,18 +78,21 @@
 
     c_copy.wait()
     c0 = c_ref[...]
-    c0_bf = c0.astype(BF16)
     half0 = 0.5 * jnp.sum(c0 * c0, axis=1, keepdims=True)
     factor = 2.0 / (scale_ref[0] * jnp.sqrt(jnp.float32(width)))
     x_copy.wait()
+    cut = [slice(h * width // 2, (h + 1) * width // 2) for h in range(2)]
     mine = pl.ds(pl.multiple_of(seq * ROWS, ROWS), ROWS)
     place = lax.broadcasted_iota(jnp.int32, (ROWS, rows), 1) == (
         seq * ROWS + lax.broadcasted_iota(jnp.int32, (ROWS, rows), 0)
     )
 
     def iteration(i, centres, half):
-        dots = lax.dot_general(
-            centres, x_ref[...], (((1,), (1,)), ((), ())), preferred_element_type=F32
+        dots = sum(
+            lax.dot_general(
+                centres[h], x_ref[:, cut[h]], (((1,), (1,)), ((), ())), preferred_element_type=F32
+            )
+            for h in range(2)
         )
         logits = factor * (dots - half)
         top = jnp.max(logits, axis=0, keepdims=True)
@@ -114,63 +117,81 @@
             jnp.ones((16, tokens), BF16), resp, (((1,), (1,)), ((), ())), preferred_element_type=F32
         )[0:1]
         mass_src[i] = mass
-        for k in range(len(SEQ)):
-            send(mass_src.at[i], mass_buf.at[i, k], m_s.at[i], m_r.at[i], peers[k])
-        w = jnp.dot(resp, x_ref[...], preferred_element_type=F32)
-        w_src[i] = w.astype(BF16)
-        for k, (z, x) in enumerate(SEQ):
-            theirs = pl.ds(pl.multiple_of(seq_index(z, x) * ROWS, ROWS), ROWS)
-            send(w_src.at[i, theirs], w_buf.at[i, k], w_s.at[i], w_r.at[i], peers[k])
-        pending.append(lambda: drain(mass_buf.at[i], m_s.at[i]))
-        pending.append(lambda: drain(w_buf.at[i], w_s.at[i]))
-        acc = w_src[i, mine, :].astype(F32)
+        for h in range(2):
+            w = jnp.dot(resp, x_ref[:, cut[h]], preferred_element_type=F32)
+            w_src[i, h] = w.astype(BF16)
+            for k, (z, x) in enumerate(SEQ):
+                theirs = pl.ds(pl.multiple_of(seq_index(z, x) * ROWS, ROWS), ROWS)
+                send(w_src.at[i, h, theirs], w_buf.at[i, h, k], w_s.at[i, h], w_r.at[i, h], peers[k])
+            pending.append(lambda h=h: drain(w_buf.at[i, h], w_s.at[i, h]))
+            if h == 0:
+                for k in range(len(SEQ)):
+                    send(mass_src.at[i], mass_buf.at[i, k], m_s.at[i], m_r.at[i], peers[k])
+                pending.append(lambda: drain(mass_buf.at[i], m_s.at[i]))
         drain(mass_buf.at[i], m_r.at[i])
         mass = mass + jnp.sum(mass_buf[i], axis=0)
-        column = jnp.sum(jnp.where(place, mass, 0.0), axis=1, keepdims=True)
-        drain(w_buf.at[i], w_r.at[i])
+        return jnp.sum(jnp.where(place, mass, 0.0), axis=1, keepdims=True) + 1.0
+
+    def summed(i, h):
+        acc = w_src[i, h, mine, :].astype(F32)
+        drain(w_buf.at[i, h], w_r.at[i, h])
         for k in range(len(SEQ)):
-            acc = acc + w_buf[i, k].astype(F32)
-        return acc, column
-
-    summed, column = iteration(0, c0_bf, half0)
-    centre = (summed + c_ref[mine, :]) / (column + 1.0)
-    own[...] = centre
-    c_next[mine, :] = centre.astype(BF16)
-    for k in range(len(SEQ)):
-        send(c_next.at[mine], c_next.at[mine], c_s, c_r, peers[k])
-    half = 0.5 * jnp.sum(centre * centre, axis=1, keepdims=True)
+            acc = acc + w_buf[i, h, k].astype(F32)
+        return acc
+
+    n_seq = len(SEQ)
+    bottom = iteration(0, [c0[:, cut[h]].astype(BF16) for h in range(2)], half0)
+    half = jnp.zeros((ROWS, 1), F32)
+    for h in range(2):
+        centre = (summed(0, h) + c_ref[mine, cut[h]]) / bottom
+        own[:, cut[h]] = centre
+        c_next[h, mine, :] = centre.astype(BF16)
+        for k in range(n_seq):
+            send(c_next.at[h, mine], c_next.at[h, mine], c_s.at[h], c_r.at[h], peers[k])
+        half += 0.5 * jnp.sum(centre * centre, axis=1, keepdims=True)
     sq_buf[seq] = jnp.sum(jnp.where(place, half, 0.0), axis=0, keepdims=True)
-    for k in range(len(SEQ)):
+    for k in range(n_seq):
         send(sq_buf.at[seq], sq_buf.at[seq], q_s, q_r, peers[k])
-    n_seq = len(SEQ)
-    blocks = c_next.at[pl.ds(0, ROWS * n_seq)]
+    blocks = [c_next.at[h, pl.ds(0, ROWS * n_seq)] for h in range(2)]
     lines = sq_buf.at[pl.ds(0, n_seq)]
-    pending.append(lambda: drain(blocks, c_s))
+    for h in range(2):
+        pending.append(lambda h=h: drain(blocks[h], c_s.at[h]))
     pending.append(lambda: drain(lines, q_s))
+    drain(blocks[0], c_r.at[0])
+    drain(blocks[1], c_r.at[1])
     drain(lines, q_r)
     line = jnp.sum(sq_buf[...], axis=0)
     diagonal = lax.broadcasted_iota(jnp.int32, (rows, rows), 0) == lax.broadcasted_iota(
         jnp.int32, (rows, rows), 1
     )
     half1 = jnp.sum(jnp.where(diagonal, line, 0.0), axis=1, keepdims=True)
-    drain(blocks, c_r)
-
-    summed, column = iteration(1, c_next[...], half1)
-    fin[0, 0] = ((summed + own[...]) / (column + 1.0)).astype(BF16)
+
+    bottom = iteration(1, [c_next[0], c_next[1]], half1)
 
     near, far = len(NEAR), len(FAR)
     slots = [1 + near + k for k in range(far)] + [1 + k for k in range(near)]
-    for k, slot in enumerate(slots):
-        g = 1 if k < far else 0
-        send(fin.at[0, 0], fin.at[0, slot], f_s.at[g], f_r.at[g], peers_chip[k])
-    parts = (fin.at[0, pl.ds(1, near)], fin.at[0, pl.ds(1 + near, far)])
+    for h in range(2):
+        fin[0, 0, :, cut[h]] = ((summed(1, h) + own[:, cut[h]]) / bottom).astype(BF16)
+        for k, slot in enumerate(slots):
+            g = 1 if k < far else 0
+            lane = pl.ds(cut[h].start, width // 2)
+            send(fin.at[0, 0, :, lane], fin.at[0, slot, :, lane], f_s.at[g, h], f_r.at[g, h], peers_chip[k])
+    first = (1, 1 + near)
+    count = (near, far)
+    parts = [
+        [fin.at[0, pl.ds(first[g], count[g]), :, pl.ds(cut[h].start, width // 2)] for h in range(2)]
+        for g in range(2)
+    ]
     halves = [[fin.at[c, pl.ds(g * (1 + near), far)] for g in range(2)] for c in range(2)]
     for g in range(2):
-        pending.append(lambda g=g: drain(parts[g], f_s.at[g]))
-    drain(parts[0], f_r.at[0])
+        for h in range(2):
+            pending.append(lambda g=g, h=h: drain(parts[g][h], f_s.at[g, h]))
+    for h in range(2):
+        drain(parts[0][h], f_r.at[0, h])
     send(halves[0][0], halves[1][0], p_s.at[0], p_r.at[0], partner)
     pending.append(lambda: drain(halves[1][0], p_s.at[0]))
-    drain(parts[1], f_r.at[1])
+    for h in range(2):
+        drain(parts[1][h], f_r.at[1, h])
     send(halves[0][1], halves[1][1], p_s.at[1], p_r.at[1], partner)
     pending.append(lambda: drain(halves[1][1], p_s.at[1]))
     pending.pop(0)()
@@ -220,15 +241,15 @@
                 pltpu.VMEM((2, 1, t), F32),
                 pltpu.VMEM((2, n_seq - 1, 1, rows), F32),
                 pltpu.VMEM((2, 1, rows), F32),
-                pltpu.VMEM((2, rows, width), BF16),
-                pltpu.VMEM((2, n_seq - 1, ROWS, width), BF16),
-                pltpu.VMEM((rows, width), BF16),
+                pltpu.VMEM((2, 2, rows, width // 2), BF16),
+                pltpu.VMEM((2, 2, n_seq - 1, ROWS, width // 2), BF16),
+                pltpu.VMEM((2, rows, width // 2), BF16),
                 pltpu.VMEM((n_seq, 1, rows), F32),
                 pltpu.VMEM((2, n_grp // 2, ROWS, width), BF16),
                 dma, dma, dma,
-                dma((2,)), dma((2,)), dma((2,)), dma((2,)), dma((2,)), dma((2,)),
-                dma, dma, dma, dma,
-                dma((2,)), dma((2,)), dma((2,)), dma((2,)),
+                dma((2,)), dma((2,)), dma((2,)), dma((2,)), dma((2, 2)), dma((2, 2)),
+                dma((2,)), dma((2,)), dma, dma,
+                dma((2, 2)), dma((2, 2)), dma((2,)), dma((2,)),
             ],
             compiler_params=pltpu.CompilerParams(
                 collective_id=0, has_side_effects=True, vmem_limit_bytes=24 * 2**20

time: 69.5 us -> 69.2 us (level)
  no operation moved by 1% of the time
where the time goes in v4:
time: 69.2 us; the launch traced here: 69 us
  Pallas kernels  67.4 us (97%)
  local copies, waits for them, and re-layouts  0.97 us (1%)
    pallas_call x1, Pallas kernels, per_device(): pl.pallas_call(kernel, out_shape=jax.ShapeDtypeStruct((n_grp, ROWS, cols)...  67.4 us

profile of v4, /device:TPU:1, one launch (start us, length us, event | category | flops | bytes accessed | tf_op | source)
XLA Modules:
  0.0 69.0 jit_solution(13461531340951413245)
XLA Ops:
  0.7 67.4 %kmeans_decode.1 = bf16[32,16,1024]{2,1,0:T(8,128)(2,1)S(1)} custom-call(bf16[512,512]{1,0:T(8,128)(2,1)} %x_hbm.1, f32[256,512]{1,0:T(8,128)} %c_hbm.1, f32[1]{0:T(128)S(6)} %copy.6.scale_ref, bf16[512,1024]{1,0:T(8,128)(2,1)} %e_hbm.1), custom_call_target="tpu_custom_call" | custom-call | tf_op jit(solution)/shard_map/kmeans_decode/pallas_call | solution.py:230
  68.1 1.0 %copy.7 = bf16[32,16,1024]{2,1,0:T(8,128)(2,1)} copy(bf16[32,16,1024]{2,1,0:T(8,128)(2,1)S(1)} %kmeans_decode.1) | data formatting | bytes 2097152

commit v5 on v4

--- a/solution.py
+++ b/solution.py
@@ -22,6 +22,7 @@
     [(z, x) for z in range(ZL) for x in range(XS) if z or x],
     key=lambda p: -(min(3, p[0]) + ring(p[1], XS)),
 )
+OCTET = [p for p in SEQ if p[0] < 2]
 NEAR = sorted([(0, y) for y in range(1, YS)], key=lambda p: -ring(p[1], YS))
 FAR = sorted([(1, y) for y in range(YS)], key=lambda p: -ring(p[1], YS))
 CHIPS = FAR + NEAR
@@ -43,14 +44,17 @@
 def kernel(
     x_hbm, c_hbm, scale_ref, e_hbm, out_ref,
     x_ref, c_ref, e_ref, own, lse_buf, lse_src, mass_buf, mass_src,
-    w_src, w_buf, c_next, sq_buf, fin,
+    mass_buf0, mass_src0, pair_mass, w_src, w_buf, w_src0, w_buf0, pair_src, pair_buf,
+    c_next, sq_buf, fin,
     x_sem, c_sem, e_sem,
-    lse_s, lse_r, m_s, m_r, w_s, w_r, c_s, c_r, q_s, q_r, f_s, f_r, p_s, p_r,
+    lse_s, lse_r, m_s, m_r, w_s, w_r, m0_s, m0_r, n_s, n_r, v_s, v_r, o_s, o_r, c_s, c_r, q_s, q_r, f_s, f_r, p_s, p_r,
 ):
     tokens, width = x_hbm.shape
     rows = c_hbm.shape[0]
     seq = lax.axis_index("seq")
     peers = [{"seq": seq_index(z, x)} for z, x in SEQ]
+    octet = [{"seq": seq_index(z, x)} for z, x in OCTET]
+    across = {"seq": seq_index(2, 0)}
     peers_chip = [{"grp": grp_index(z, y, 0)} for z, y in CHIPS]
     peers_other = [{"grp": grp_index(z, y, 1)} for z, y in CHIPS]
     partner = {"grp": grp_index(0, 0, 1)}
@@ -83,11 +87,8 @@
     x_copy.wait()
     cut = [slice(h * width // 2, (h + 1) * width // 2) for h in range(2)]
     mine = pl.ds(pl.multiple_of(seq * ROWS, ROWS), ROWS)
-    place = lax.broadcasted_iota(jnp.int32, (ROWS, rows), 1) == (
-        seq * ROWS + lax.broadcasted_iota(jnp.int32, (ROWS, rows), 0)
-    )
-
-    def iteration(i, centres, half):
+
+    def softmax(i, centres, half):
         dots = sum(
             lax.dot_general(
                 centres[h], x_ref[:, cut[h]], (((1,), (1,)), ((), ())), preferred_element_type=F32
@@ -116,44 +117,63 @@
         mass = lax.dot_general(
             jnp.ones((16, tokens), BF16), resp, (((1,), (1,)), ((), ())), preferred_element_type=F32
         )[0:1]
-        mass_src[i] = mass
-        for h in range(2):
-            w = jnp.dot(resp, x_ref[:, cut[h]], preferred_element_type=F32)
-            w_src[i, h] = w.astype(BF16)
-            for k, (z, x) in enumerate(SEQ):
-                theirs = pl.ds(pl.multiple_of(seq_index(z, x) * ROWS, ROWS), ROWS)
-                send(w_src.at[i, h, theirs], w_buf.at[i, h, k], w_s.at[i, h], w_r.at[i, h], peers[k])
-            pending.append(lambda h=h: drain(w_buf.at[i, h], w_s.at[i, h]))
-            if h == 0:
-                for k in range(len(SEQ)):
-                    send(mass_src.at[i], mass_buf.at[i, k], m_s.at[i], m_r.at[i], peers[k])
-                pending.append(lambda: drain(mass_buf.at[i], m_s.at[i]))
-        drain(mass_buf.at[i], m_r.at[i])
-        mass = mass + jnp.sum(mass_buf[i], axis=0)
-        return jnp.sum(jnp.where(place, mass, 0.0), axis=1, keepdims=True) + 1.0
-
-    def summed(i, h):
-        acc = w_src[i, h, mine, :].astype(F32)
-        drain(w_buf.at[i, h], w_r.at[i, h])
-        for k in range(len(SEQ)):
-            acc = acc + w_buf[i, h, k].astype(F32)
-        return acc
-
-    n_seq = len(SEQ)
-    bottom = iteration(0, [c0[:, cut[h]].astype(BF16) for h in range(2)], half0)
-    half = jnp.zeros((ROWS, 1), F32)
-    for h in range(2):
-        centre = (summed(0, h) + c_ref[mine, cut[h]]) / bottom
-        own[:, cut[h]] = centre
-        c_next[h, mine, :] = centre.astype(BF16)
-        for k in range(n_seq):
-            send(c_next.at[h, mine], c_next.at[h, mine], c_s.at[h], c_r.at[h], peers[k])
-        half += 0.5 * jnp.sum(centre * centre, axis=1, keepdims=True)
-    sq_buf[seq] = jnp.sum(jnp.where(place, half, 0.0), axis=0, keepdims=True)
-    for k in range(n_seq):
-        send(sq_buf.at[seq], sq_buf.at[seq], q_s, q_r, peers[k])
-    blocks = [c_next.at[h, pl.ds(0, ROWS * n_seq)] for h in range(2)]
-    lines = sq_buf.at[pl.ds(0, n_seq)]
+        return resp, mass
+
+    n_oct = len(OCTET)
+    j = seq % 8
+    block = pl.ds(pl.multiple_of(j * ROWS, ROWS), ROWS)
+    resp, mass = softmax(0, [c0[:, cut[h]].astype(BF16) for h in range(2)], half0)
+    mass_src0[0] = mass
+    for h in range(2):
+        w = jnp.dot(resp, x_ref[:, cut[h]], preferred_element_type=F32)
+        w_src0[h] = w.astype(BF16).reshape(2, rows // 2, width // 2)
+        for k, (z, x) in enumerate(OCTET):
+            theirs = pl.ds(pl.multiple_of((seq_index(z, x) % 8) * ROWS, ROWS), ROWS)
+            send(w_src0.at[h, :, theirs], w_buf0.at[h, k], v_s.at[h], v_r.at[h], octet[k])
+        pending.append(lambda h=h: drain(w_buf0.at[h], v_s.at[h]))
+        if h == 0:
+            for k in range(n_oct):
+                send(mass_src0.at[0], mass_buf0.at[k], m0_s, m0_r, octet[k])
+            pending.append(lambda: drain(mass_buf0, m0_s))
+    for h in range(2):
+        acc = w_src0[h, :, block, :].astype(F32)
+        drain(w_buf0.at[h], v_r.at[h])
+        for k in range(n_oct):
+            acc = acc + w_buf0[h, k].astype(F32)
+        pair_src[h] = acc.astype(BF16)
+        send(pair_src.at[h], pair_buf.at[h], o_s.at[h], o_r.at[h], across)
+        pending.append(lambda h=h: drain(pair_buf.at[h], o_s.at[h]))
+        if h == 0:
+            drain(mass_buf0, m0_r)
+            mass = mass + jnp.sum(mass_buf0[...], axis=0)
+            mass_src0[1] = mass
+            send(mass_src0.at[1], pair_mass, n_s, n_r, across)
+            pending.append(lambda: drain(pair_mass, n_s))
+    drain(pair_mass, n_r)
+    mass = mass + pair_mass[...]
+    lane = lax.broadcasted_iota(jnp.int32, (ROWS, rows), 1)
+    row = lax.broadcasted_iota(jnp.int32, (ROWS, rows), 0)
+    spots = [lane == hi * (rows // 2) + j * ROWS + row for hi in range(2)]
+    bottoms = [jnp.sum(jnp.where(s, mass, 0.0), axis=1, keepdims=True) + 1.0 for s in spots]
+    halves = [jnp.zeros((ROWS, 1), F32) for _ in range(2)]
+    for h in range(2):
+        drain(pair_buf.at[h], o_r.at[h])
+        for hi in range(2):
+            start = c_ref[pl.ds(pl.multiple_of(hi * (rows // 2) + j * ROWS, ROWS), ROWS), cut[h]]
+            both = pair_src[h, hi].astype(F32) + pair_buf[h, hi].astype(F32)
+            centre = (both + start) / bottoms[hi]
+            own[hi, :, cut[h]] = centre
+            c_next[h, hi, block, :] = centre.astype(BF16)
+            halves[hi] += 0.5 * jnp.sum(centre * centre, axis=1, keepdims=True)
+        for k in range(n_oct):
+            send(c_next.at[h, :, block], c_next.at[h, :, block], c_s.at[h], c_r.at[h], octet[k])
+    sq_buf[j] = sum(
+        jnp.sum(jnp.where(spots[hi], halves[hi], 0.0), axis=0, keepdims=True) for hi in range(2)
+    )
+    for k in range(n_oct):
+        send(sq_buf.at[j], sq_buf.at[j], q_s, q_r, octet[k])
+    blocks = [c_next.at[h, :, pl.ds(0, ROWS * n_oct)] for h in range(2)]
+    lines = sq_buf.at[pl.ds(0, n_oct)]
     for h in range(2):
         pending.append(lambda h=h: drain(blocks[h], c_s.at[h]))
     pending.append(lambda: drain(lines, q_s))
@@ -166,12 +186,34 @@
     )
     half1 = jnp.sum(jnp.where(diagonal, line, 0.0), axis=1, keepdims=True)
 
-    bottom = iteration(1, [c_next[0], c_next[1]], half1)
+    resp, mass = softmax(1, [c_next[h].reshape(rows, width // 2) for h in range(2)], half1)
+    mass_src[...] = mass
+    for h in range(2):
+        w = jnp.dot(resp, x_ref[:, cut[h]], preferred_element_type=F32)
+        w_src[h] = w.astype(BF16)
+        for k, (z, x) in enumerate(SEQ):
+            theirs = pl.ds(pl.multiple_of(seq_index(z, x) * ROWS, ROWS), ROWS)
+            send(w_src.at[h, theirs], w_buf.at[h, k], w_s.at[h], w_r.at[h], peers[k])
+        pending.append(lambda h=h: drain(w_buf.at[h], w_s.at[h]))
+        if h == 0:
+            for k in range(len(SEQ)):
+                send(mass_src, mass_buf.at[k], m_s, m_r, peers[k])
+            pending.append(lambda: drain(mass_buf, m_s))
+    drain(mass_buf, m_r)
+    mass = mass + jnp.sum(mass_buf[...], axis=0)
+    bottom = jnp.sum(jnp.where(lane == seq * ROWS + row, mass, 0.0), axis=1, keepdims=True) + 1.0
+
+    def summed(h):
+        acc = w_src[h, mine, :].astype(F32)
+        drain(w_buf.at[h], w_r.at[h])
+        for k in range(len(SEQ)):
+            acc = acc + w_buf[h, k].astype(F32)
+        return acc
 
     near, far = len(NEAR), len(FAR)
     slots = [1 + near + k for k in range(far)] + [1 + k for k in range(near)]
     for h in range(2):
-        fin[0, 0, :, cut[h]] = ((summed(1, h) + own[:, cut[h]]) / bottom).astype(BF16)
+        fin[0, 0, :, cut[h]] = ((summed(h) + own[seq // 8, :, cut[h]]) / bottom).astype(BF16)
         for k, slot in enumerate(slots):
             g = 1 if k < far else 0
             lane = pl.ds(cut[h].start, width // 2)
@@ -182,18 +224,18 @@
         [fin.at[0, pl.ds(first[g], count[g]), :, pl.ds(cut[h].start, width // 2)] for h in range(2)]
         for g in range(2)
     ]
-    halves = [[fin.at[c, pl.ds(g * (1 + near), far)] for g in range(2)] for c in range(2)]
+    sides = [[fin.at[c, pl.ds(g * (1 + near), far)] for g in range(2)] for c in range(2)]
     for g in range(2):
         for h in range(2):
             pending.append(lambda g=g, h=h: drain(parts[g][h], f_s.at[g, h]))
     for h in range(2):
         drain(parts[0][h], f_r.at[0, h])
-    send(halves[0][0], halves[1][0], p_s.at[0], p_r.at[0], partner)
-    pending.append(lambda: drain(halves[1][0], p_s.at[0]))
+    send(sides[0][0], sides[1][0], p_s.at[0], p_r.at[0], partner)
+    pending.append(lambda: drain(sides[1][0], p_s.at[0]))
     for h in range(2):
         drain(parts[1][h], f_r.at[1, h])
-    send(halves[0][1], halves[1][1], p_s.at[1], p_r.at[1], partner)
-    pending.append(lambda: drain(halves[1][1], p_s.at[1]))
+    send(sides[0][1], sides[1][1], p_s.at[1], p_r.at[1], partner)
+    pending.append(lambda: drain(sides[1][1], p_s.at[1]))
     pending.pop(0)()
     me = lax.axis_index("grp")
     mc, my, mz = me % CORES, (me // CORES) % YS, me // (CORES * YS)
@@ -208,9 +250,9 @@
             out_ref[g] = d[k * ROWS : (k + 1) * ROWS]
 
     decode(0, 0, 2 * far)
-    drain(halves[1][0], p_r.at[0])
+    drain(sides[1][0], p_r.at[0])
     decode(1, 0, far)
-    drain(halves[1][1], p_r.at[1])
+    drain(sides[1][1], p_r.at[1])
     decode(1, far, far)
 
     for wait in pending:
@@ -224,6 +266,7 @@
         cols = e.shape[1]
         n_grp = ZH * YS * CORES
         n_seq = XS * ZL
+        n_oct = len(OCTET)
         hbm = pl.BlockSpec(memory_space=pltpu.HBM)
         dma = pltpu.SemaphoreType.DMA
         x, c, e = (pltpu.with_memory_space_constraint(v, pltpu.HBM) for v in (x, c, e))
@@ -236,18 +279,26 @@
                 pltpu.VMEM((t, width), BF16),
                 pltpu.VMEM((rows, width), F32),
                 pltpu.VMEM((width, cols), BF16),
-                pltpu.VMEM((ROWS, width), F32),
+                pltpu.VMEM((2, ROWS, width), F32),
                 pltpu.VMEM((2, n_grp - 1, 1, t), F32),
                 pltpu.VMEM((2, 1, t), F32),
-                pltpu.VMEM((2, n_seq - 1, 1, rows), F32),
+                pltpu.VMEM((n_seq - 1, 1, rows), F32),
+                pltpu.VMEM((1, rows), F32),
+                pltpu.VMEM((n_oct, 1, rows), F32),
                 pltpu.VMEM((2, 1, rows), F32),
-                pltpu.VMEM((2, 2, rows, width // 2), BF16),
-                pltpu.VMEM((2, 2, n_seq - 1, ROWS, width // 2), BF16),
+                pltpu.VMEM((1, rows), F32),
                 pltpu.VMEM((2, rows, width // 2), BF16),
-                pltpu.VMEM((n_seq, 1, rows), F32),
+                pltpu.VMEM((2, n_seq - 1, ROWS, width // 2), BF16),
+                pltpu.VMEM((2, 2, rows // 2, width // 2), BF16),
+                pltpu.VMEM((2, n_oct, 2, ROWS, width // 2), BF16),
+                pltpu.VMEM((2, 2, ROWS, width // 2), BF16),
+                pltpu.VMEM((2, 2, ROWS, width // 2), BF16),
+                pltpu.VMEM((2, 2, rows // 2, width // 2), BF16),
+                pltpu.VMEM((n_oct + 1, 1, rows), F32),
                 pltpu.VMEM((2, n_grp // 2, ROWS, width), BF16),
                 dma, dma, dma,
-                dma((2,)), dma((2,)), dma((2,)), dma((2,)), dma((2, 2)), dma((2, 2)),
+                dma((2,)), dma((2,)), dma, dma, dma((2,)), dma((2,)),
+                dma, dma, dma, dma, dma((2,)), dma((2,)), dma((2,)), dma((2,)),
                 dma((2,)), dma((2,)), dma, dma,
                 dma((2, 2)), dma((2, 2)), dma((2,)), dma((2,)),
             ],

time: 69.2 us -> 67.4 us (0.974)
  Pallas kernels: 67.4 us -> 65.6 us
    pallas_call x1, Pallas kernels: 67.4 us -> 65.6 us  [per_device(): pl.pallas_call(kernel, out_shape=jax.ShapeDtypeStruct((n_grp, ROWS, cols)...]
where the time goes in v5:
time: 67.4 us; the launch traced here: 67.3 us
  Pallas kernels  65.6 us (97%)
  local copies, waits for them, and re-layouts  0.97 us (1%)
    pallas_call x1, Pallas kernels, per_device(): pl.pallas_call(kernel, out_shape=jax.ShapeDtypeStruct((n_grp, ROWS, cols)...  65.6 us

profile of v5, /device:TPU:1, one launch (start us, length us, event | category | flops | bytes accessed | tf_op | source)
XLA Modules:
  0.0 67.3 jit_solution(1252109944053205529)
XLA Ops:
  0.7 65.6 %kmeans_decode.1 = bf16[32,16,1024]{2,1,0:T(8,128)(2,1)S(1)} custom-call(bf16[512,512]{1,0:T(8,128)(2,1)} %x_hbm.1, f32[256,512]{1,0:T(8,128)} %c_hbm.1, f32[1]{0:T(128)S(6)} %copy.6.scale_ref, bf16[512,1024]{1,0:T(8,128)(2,1)} %e_hbm.1), custom_call_target="tpu_custom_call" | custom-call | tf_op jit(solution)/shard_map/kmeans_decode/pallas_call | solution.py:273
  66.3 1.0 %copy.7 = bf16[32,16,1024]{2,1,0:T(8,128)(2,1)} copy(bf16[32,16,1024]{2,1,0:T(8,128)(2,1)S(1)} %kmeans_decode.1) | data formatting | bytes 2097152

commit v6 on v4

v6 whole, which is shorter than its diff:
```python
import functools

import jax
import jax.numpy as jnp
from jax import lax
from jax.experimental import pallas as pl
from jax.experimental.pallas import tpu as pltpu
from jax.sharding import PartitionSpec as P

MESH = pl.DeviceIdType.MESH
XS, ZL = 4, 4
ZH, YS, CORES = 2, 8, 2
ROWS = 16
F32, BF16 = jnp.float32, jnp.bfloat16


def ring(d, n):
    return min(d, n - d)


OCTET = sorted(
    [(z, x) for z in range(2) for x in range(XS) if z or x], key=lambda p: -(p[0] + ring(p[1], XS))
)
NEAR = sorted([(0, y) for y in range(1, YS)], key=lambda p: -ring(p[1], YS))
FAR = sorted([(1, y) for y in range(YS)], key=lambda p: -ring(p[1], YS))
CHIPS = FAR + NEAR


def seq_index(z, x):
    me = lax.axis_index("seq")
    mz, mx = me // XS, me % XS
    pz = ((mz // 2 + z // 2) % 2) * 2 + (mz % 2 + z % 2) % 2
    return pz * XS + (mx + x) % XS


def grp_index(z, y, c):
    me = lax.axis_index("grp")
    mc, my, mz = me % CORES, (me // CORES) % YS, me // (CORES * YS)
    return (((mz + z) % ZH) * YS + (my + y) % YS) * CORES + (mc + c) % CORES


def kernel(
    x_hbm, c_hbm, scale_ref, e_hbm, out_ref,
    x_ref, c_ref, e_ref, own, lse_buf, lse_src, mass_buf, mass_src, pair_mass,
    w_src, w_buf, pair_src, pair_buf, last_src, last_buf, c_src, c_next, sq_src, sq_buf, fin,
    x_sem, c_sem, e_sem,
    lse_s, lse_r, m_s, m_r, n_s, n_r, w_s, w_r, o_s, o_r, l_s, l_r,
    c_s, c_r, q_s, q_r, f_s, f_r, p_s, p_r,
):
    tokens, width = x_hbm.shape
    rows = c_hbm.shape[0]
    seq = lax.axis_index("seq")
    partner_group = grp_index(0, 0, 1)
    octet = [{"seq": seq_index(z, x), "grp": partner_group} for z, x in OCTET] + [{"grp": partner_group}]
    octet_index = [seq_index(z, x) % 8 for z, x in OCTET] + [seq % 8]
    across = {"seq": seq_index(2, 0)}
    peers_chip = [{"grp": grp_index(z, y, 0)} for z, y in CHIPS]
    peers_other = [{"grp": grp_index(z, y, 1)} for z, y in CHIPS]
    partner = {"grp": partner_group}
    everyone = [p for pair in zip(peers_chip, peers_other) for p in pair] + octet + [across]

    c_copy = pltpu.make_async_copy(c_hbm, c_ref, c_sem)
    c_copy.start()
    x_copy = pltpu.make_async_copy(x_hbm, x_ref, x_sem)
    x_copy.start()
    barrier = pltpu.get_barrier_semaphore()
    for p in everyone:
        pl.semaphore_signal(barrier, inc=1, device_id=p, device_id_type=MESH)
    e_copy = pltpu.make_async_copy(e_hbm, e_ref, e_sem)
    e_copy.start()
    pending = [e_copy.wait]

    def send(src, dst, ssem, rsem, device):
        pltpu.make_async_remote_copy(
            src_ref=src, dst_ref=dst, send_sem=ssem, recv_sem=rsem,
            device_id=device, device_id_type=MESH,
        ).start()

    def drain(ref, sem):
        pltpu.make_async_copy(ref, ref, sem).wait()

    c_copy.wait()
    c0 = c_ref[...]
    half0 = 0.5 * jnp.sum(c0 * c0, axis=1, keepdims=True)
    factor = 2.0 / (scale_ref[0] * jnp.sqrt(jnp.float32(width)))
    x_copy.wait()
    cut = [slice(h * width // 2, (h + 1) * width // 2) for h in range(2)]

    def softmax(i, centres, half):
        dots = sum(
            lax.dot_general(
                centres[h], x_ref[:, cut[h]], (((1,), (1,)), ((), ())), preferred_element_type=F32
            )
            for h in range(2)
        )
        logits = factor * (dots - half)
        top = jnp.max(logits, axis=0, keepdims=True)
        lse = top + jnp.log(jnp.sum(jnp.exp(logits - top), axis=0, keepdims=True))
        lse_src[i] = lse
        if i == 0:
            pl.semaphore_wait(barrier, len(everyone))
        slot = 0
        for a, b in zip(peers_chip, peers_other):
            for p in (a, b):
                send(lse_src.at[i], lse_buf.at[i, slot], lse_s.at[i], lse_r.at[i], p)
                slot += 1
        send(lse_src.at[i], lse_buf.at[i, slot], lse_s.at[i], lse_r.at[i], partner)
        pending.append(lambda: drain(lse_buf.at[i], lse_s.at[i]))
        drain(lse_buf.at[i], lse_r.at[i])
        others = lse_buf[i]
        m = jnp.maximum(jnp.max(others, axis=0), lse)
        total = jnp.sum(jnp.exp(others - m[None]), axis=0) + jnp.exp(lse - m)
        full = m + jnp.log(total)
        resp = jnp.exp(logits - full).astype(BF16)
        mass = lax.dot_general(
            jnp.ones((16, tokens), BF16), resp, (((1,), (1,)), ((), ())), preferred_element_type=F32
        )[0:1]
        return resp, mass

    n_oct = len(octet)
    j, hi = seq % 8, seq // 8
    lane = lax.broadcasted_iota(jnp.int32, (ROWS, rows), 1)
    row = lax.broadcasted_iota(jnp.int32, (ROWS, rows), 0)
    spots = [lane == q * (rows // 2) + j * ROWS + row for q in range(2)]

    def scatter(i, resp, mass):
        mass_src[i, 0] = mass
        for h in range(2):
            w = jnp.dot(resp, x_ref[:, cut[h]], preferred_element_type=F32)
            w_src[i, h] = w.astype(BF16).reshape(2, rows // 2, width // 2)
            if i == 0:
                mine = pl.ds(pl.multiple_of(j * ROWS, ROWS), ROWS)
                w_src[0, h, hi, mine, :] = (
                    w_src[0, h, hi, mine, :].astype(F32)
                    + c_ref[pl.ds(pl.multiple_of(seq * ROWS, ROWS), ROWS), cut[h]]
                ).astype(BF16)
            for k in range(n_oct):
                theirs = pl.ds(pl.multiple_of(octet_index[k] * ROWS, ROWS), ROWS)
                send(w_src.at[i, h, :, theirs], w_buf.at[i, h, k], w_s.at[i, h], w_r.at[i, h], octet[k])
            pending.append(lambda h=h: drain(w_buf.at[i, h], w_s.at[i, h]))
            if h == 0:
                for k in range(n_oct):
                    send(mass_src.at[i, 0], mass_buf.at[i, k], m_s.at[i], m_r.at[i], octet[k])
                pending.append(lambda: drain(mass_buf.at[i], m_s.at[i]))

    def partial(i, h, side):
        acc = w_buf[i, h, 0, side].astype(F32)
        for k in range(1, n_oct):
            acc = acc + w_buf[i, h, k, side].astype(F32)
        return acc

    def pair_up_mass(i):
        drain(mass_buf.at[i], m_r.at[i])
        mass = jnp.sum(mass_buf[i], axis=0)
        mass_src[i, 1] = mass
        send(mass_src.at[i, 1], pair_mass.at[i], n_s.at[i], n_r.at[i], across)
        pending.append(lambda: drain(pair_mass.at[i], n_s.at[i]))
        return mass

    scatter(0, *softmax(0, [c0[:, cut[h]].astype(BF16) for h in range(2)], half0))
    for h in range(2):
        drain(w_buf.at[0, h], w_r.at[0, h])
        for q in range(2):
            pair_src[h, q] = partial(0, h, q).astype(BF16)
        send(pair_src.at[h], pair_buf.at[h], o_s.at[h], o_r.at[h], across)
        pending.append(lambda h=h: drain(pair_buf.at[h], o_s.at[h]))
        if h == 0:
            mass = pair_up_mass(0)
    drain(pair_mass.at[0], n_r.at[0])
    mass = mass + pair_mass[0]
    bottoms = [jnp.sum(jnp.where(s, mass, 0.0), axis=1, keepdims=True) + 1.0 for s in spots]
    halves = [jnp.zeros((ROWS, 1), F32) for _ in range(2)]
    block = pl.ds(pl.multiple_of(j * ROWS, ROWS), ROWS)
    for h in range(2):
        drain(pair_buf.at[h], o_r.at[h])
        for q in range(2):
            both = pair_src[h, q].astype(F32) + pair_buf[h, q].astype(F32)
            centre = both / bottoms[q]
            own[q, :, cut[h]] = centre
            c_src[h, q] = centre.astype(BF16)
            halves[q] += 0.5 * jnp.sum(centre * centre, axis=1, keepdims=True)
        for k in range(n_oct):
            send(c_src.at[h], c_next.at[h, :, block], c_s.at[h], c_r.at[h], octet[k])
        pending.append(lambda h=h: drain(c_next.at[h], c_s.at[h]))
    sq_src[...] = sum(
        jnp.sum(jnp.where(spots[q], halves[q], 0.0), axis=0, keepdims=True) for q in range(2)
    )
    for k in range(n_oct):
        send(sq_src, sq_buf.at[j], q_s, q_r, octet[k])
    pending.append(lambda: drain(sq_buf, q_s))
    drain(c_next.at[0], c_r.at[0])
    drain(c_next.at[1], c_r.at[1])
    drain(sq_buf, q_r)
    line = jnp.sum(sq_buf[...], axis=0)
    diagonal = lax.broadcasted_iota(jnp.int32, (rows, rows), 0) == lax.broadcasted_iota(
        jnp.int32, (rows, rows), 1
    )
    half1 = jnp.sum(jnp.where(diagonal, line, 0.0), axis=1, keepdims=True)

    scatter(1, *softmax(1, [c_next[h].reshape(rows, width // 2) for h in range(2)], half1))
    kept = []
    for h in range(2):
        drain(w_buf.at[1, h], w_r.at[1, h])
        last_src[h] = partial(1, h, 1 - hi).astype(BF16)
        send(last_src.at[h], last_buf.at[h], l_s.at[h], l_r.at[h], across)
        pending.append(lambda h=h: drain(last_buf.at[h], l_s.at[h]))
        kept.append(partial(1, h, hi))
        if h == 0:
            mass = pair_up_mass(1)
    drain(pair_mass.at[1], n_r.at[1])
    mass = mass + pair_mass[1]
    bottom = jnp.sum(jnp.where(lane == seq * ROWS + row, mass, 0.0), axis=1, keepdims=True) + 1.0

    def summed(h):
        drain(last_buf.at[h], l_r.at[h])
        return kept[h] + last_buf[h].astype(F32)

    near, far = len(NEAR), len(FAR)
    slots = [1 + near + k for k in range(far)] + [1 + k for k in range(near)]
    first, count = (1, 1 + near), (near, far)
    for h in range(2):
        fin[1, 0, :, cut[h]] = ((summed(h) + own[hi, :, cut[h]]) / bottom).astype(BF16)
        for k, slot in enumerate(slots):
            g = 1 if k < far else 0
            lanes = pl.ds(cut[h].start, width // 2)
            send(fin.at[1, 0, :, lanes], fin.at[0, slot, :, lanes], f_s.at[g, h], f_r.at[g, h], peers_other[k])
    send(fin.at[1, 0], fin.at[0, 0], p_s.at[0], p_r.at[0], partner)
    pending.append(lambda: drain(fin.at[0, 0], p_s.at[0]))
    parts = [
        [fin.at[0, pl.ds(first[g], count[g]), :, pl.ds(cut[h].start, width // 2)] for h in range(2)]
        for g in range(2)
    ]
    sides = [[fin.at[c, pl.ds(first[g], count[g])] for g in range(2)] for c in range(2)]
    for g in range(2):
        for h in range(2):
            pending.append(lambda g=g, h=h: drain(parts[g][h], f_s.at[g, h]))
    for g in range(2):
        for h in range(2):
            drain(parts[g][h], f_r.at[g, h])
        send(sides[0][g], sides[1][g], p_s.at[g + 1], p_r.at[g + 1], partner)
        pending.append(lambda g=g: drain(sides[1][g], p_s.at[g + 1]))
    pending.pop(0)()
    drain(fin.at[0, 0], p_r.at[0])
    me = lax.axis_index("grp")
    mc, my, mz = me % CORES, (me // CORES) % YS, me // (CORES * YS)
    chips = [(0, 0)] + NEAR + FAR

    def decode(half, first, count):
        part = fin[half, first : first + count].reshape(count * ROWS, width)
        d = jnp.dot(part, e_ref[...], preferred_element_type=F32).astype(BF16)
        for k in range(count):
            z, y = chips[first + k]
            g = (((mz + ZH - z) % ZH) * YS + (my + YS - y) % YS) * CORES + (mc + half) % CORES
            out_ref[g] = d[k * ROWS : (k + 1) * ROWS]

    decode(0, 0, 2 * far)
    drain(sides[1][0], p_r.at[1])
    decode(1, 0, far)
    drain(sides[1][1], p_r.at[2])
    decode(1, far, far)

    for wait in pending:
        wait()


def solution(mesh):
    def per_device(x, c, scale, e):
        t, width = x.shape
        rows = c.shape[0]
        cols = e.shape[1]
        n_grp = ZH * YS * CORES
        n_oct = len(OCTET) + 1
        hbm = pl.BlockSpec(memory_space=pltpu.HBM)
        dma = pltpu.SemaphoreType.DMA
        x, c, e = (pltpu.with_memory_space_constraint(v, pltpu.HBM) for v in (x, c, e))
        return pl.pallas_call(
            kernel,
            out_shape=jax.ShapeDtypeStruct((n_grp, ROWS, cols), BF16),
            in_specs=[hbm, hbm, pl.BlockSpec(memory_space=pltpu.SMEM), hbm],
            out_specs=pl.BlockSpec(memory_space=pltpu.VMEM),
            scratch_shapes=[
                pltpu.VMEM((t, width), BF16),
                pltpu.VMEM((rows, width), F32),
                pltpu.VMEM((width, cols), BF16),
                pltpu.VMEM((2, ROWS, width), F32),
                pltpu.VMEM((2, n_grp - 1, 1, t), F32),
                pltpu.VMEM((2, 1, t), F32),
                pltpu.VMEM((2, n_oct, 1, rows), F32),
                pltpu.VMEM((2, 2, 1, rows), F32),
                pltpu.VMEM((2, 1, rows), F32),
                pltpu.VMEM((2, 2, 2, rows // 2, width // 2), BF16),
                pltpu.VMEM((2, 2, n_oct, 2, ROWS, width // 2), BF16),
                pltpu.VMEM((2, 2, ROWS, width // 2), BF16),
                pltpu.VMEM((2, 2, ROWS, width // 2), BF16),
                pltpu.VMEM((2, ROWS, width // 2), BF16),
                pltpu.VMEM((2, ROWS, width // 2), BF16),
                pltpu.VMEM((2, 2, ROWS, width // 2), BF16),
                pltpu.VMEM((2, 2, rows // 2, width // 2), BF16),
                pltpu.VMEM((1, rows), F32),
                pltpu.VMEM((n_oct, 1, rows), F32),
                pltpu.VMEM((2, n_grp // 2, ROWS, width), BF16),
                dma, dma, dma,
                dma((2,)), dma((2,)), dma((2,)), dma((2,)), dma((2,)), dma((2,)),
                dma((2, 2)), dma((2, 2)), dma((2,)), dma((2,)), dma((2,)), dma((2,)),
                dma((2,)), dma((2,)), dma, dma,
                dma((2, 2)), dma((2, 2)), dma((3,)), dma((3,)),
            ],
            compiler_params=pltpu.CompilerParams(
                collective_id=0, has_side_effects=True, vmem_limit_bytes=24 * 2**20
            ),
            name="kmeans_decode",
        )(x, c, scale, e)

    placed = (P("seq", None), P("grp", None), P(), P(None, "grp"))
    return jax.shard_map(
        per_device, mesh=mesh, in_specs=placed, out_specs=P(None, "seq", "grp"), check_vma=False
    )
```

time: 69.2 us -> 64.9 us (0.938)
  Pallas kernels: 67.4 us -> 63.2 us
    pallas_call x1, Pallas kernels: 67.4 us -> 63.2 us  [per_device(): pl.pallas_call(kernel, out_shape=jax.ShapeDtypeStruct((n_grp, ROWS, cols)...]
where the time goes in v6:
time: 64.9 us; the launch traced here: 64.8 us
  Pallas kernels  63.2 us (97%)
  local copies, waits for them, and re-layouts  0.97 us (1%)
  between operations  0.66 us (1%)
    pallas_call x1, Pallas kernels, per_device(): pl.pallas_call(kernel, out_shape=jax.ShapeDtypeStruct((n_grp, ROWS, cols)...  63.2 us

profile of v6, /device:TPU:1, one launch (start us, length us, event | category | flops | bytes accessed | tf_op | source)
XLA Modules:
  0.0 64.8 jit_solution(17362919020661853796)
XLA Ops:
  0.7 63.2 %kmeans_decode.1 = bf16[32,16,1024]{2,1,0:T(8,128)(2,1)S(1)} custom-call(bf16[512,512]{1,0:T(8,128)(2,1)} %x_hbm.1, f32[256,512]{1,0:T(8,128)} %c_hbm.1, f32[1]{0:T(128)S(6)} %copy.6.scale_ref, bf16[512,1024]{1,0:T(8,128)(2,1)} %e_hbm.1), custom_call_target="tpu_custom_call" | custom-call | tf_op jit(solution)/shard_map/kmeans_decode/pallas_call | solution.py:276
  63.8 1.0 %copy.7 = bf16[32,16,1024]{2,1,0:T(8,128)(2,1)} copy(bf16[32,16,1024]{2,1,0:T(8,128)(2,1)S(1)} %kmeans_decode.1) | data formatting | bytes 2097152

commit v7 on v6

--- a/solution.py
+++ b/solution.py
@@ -12,6 +12,7 @@
 ZH, YS, CORES = 2, 8, 2
 ROWS = 16
 F32, BF16 = jnp.float32, jnp.bfloat16
+PIECES = (2, 2)
 
 
 def ring(d, n):
@@ -41,14 +42,15 @@
 
 def kernel(
     x_hbm, c_hbm, scale_ref, e_hbm, out_ref,
-    x_ref, c_ref, e_ref, own, lse_buf, lse_src, mass_buf, mass_src, pair_mass,
-    w_src, w_buf, pair_src, pair_buf, last_src, last_buf, c_src, c_next, sq_src, sq_buf, fin,
-    x_sem, c_sem, e_sem,
+    x_ref, c_ref, e_ref, own, theirs_c, lse_buf, lse_src, mass_buf, mass_src, pair_mass,
+    w_src0, w_src1, w_buf0, w_buf1, pair_src, pair_buf, last_src, last_buf, c_src, c_next, sq_src, sq_buf, fin,
+    x_sem, c_sem, e_sem, a_s, a_r,
     lse_s, lse_r, m_s, m_r, n_s, n_r, w_s, w_r, o_s, o_r, l_s, l_r,
-    c_s, c_r, q_s, q_r, f_s, f_r, p_s, p_r,
+    c_s, c_r, q_s, q_r, f_s, f_r, p_s, p_r, h_s, h_r,
 ):
     tokens, width = x_hbm.shape
     rows = c_hbm.shape[0]
+    w_src, w_buf = (w_src0, w_src1), (w_buf0, w_buf1)
     seq = lax.axis_index("seq")
     partner_group = grp_index(0, 0, 1)
     octet = [{"seq": seq_index(z, x), "grp": partner_group} for z, x in OCTET] + [{"grp": partner_group}]
@@ -84,14 +86,15 @@
     half0 = 0.5 * jnp.sum(c0 * c0, axis=1, keepdims=True)
     factor = 2.0 / (scale_ref[0] * jnp.sqrt(jnp.float32(width)))
     x_copy.wait()
-    cut = [slice(h * width // 2, (h + 1) * width // 2) for h in range(2)]
+    size = [width // n for n in PIECES]
+    cuts = [[slice(h * size[i], (h + 1) * size[i]) for h in range(n)] for i, n in enumerate(PIECES)]
 
     def softmax(i, centres, half):
         dots = sum(
             lax.dot_general(
-                centres[h], x_ref[:, cut[h]], (((1,), (1,)), ((), ())), preferred_element_type=F32
+                centres[h], x_ref[:, cuts[0][h]], (((1,), (1,)), ((), ())), preferred_element_type=F32
             )
-            for h in range(2)
+            for h in range(PIECES[0])
         )
         logits = factor * (dots - half)
         top = jnp.max(logits, axis=0, keepdims=True)
@@ -106,16 +109,18 @@
                 slot += 1
         send(lse_src.at[i], lse_buf.at[i, slot], lse_s.at[i], lse_r.at[i], partner)
         pending.append(lambda: drain(lse_buf.at[i], lse_s.at[i]))
+        if i == 0:
+            for q in range(2):
+                start = pl.ds(pl.multiple_of(q * (rows // 2) + (seq % 8) * ROWS, ROWS), ROWS)
+                send(c_ref.at[start], theirs_c.at[q], a_s, a_r, partner)
+            pending.append(lambda: drain(theirs_c, a_s))
         drain(lse_buf.at[i], lse_r.at[i])
         others = lse_buf[i]
         m = jnp.maximum(jnp.max(others, axis=0), lse)
         total = jnp.sum(jnp.exp(others - m[None]), axis=0) + jnp.exp(lse - m)
         full = m + jnp.log(total)
         resp = jnp.exp(logits - full).astype(BF16)
-        mass = lax.dot_general(
-            jnp.ones((16, tokens), BF16), resp, (((1,), (1,)), ((), ())), preferred_element_type=F32
-        )[0:1]
-        return resp, mass
+        return resp
 
     n_oct = len(octet)
     j, hi = seq % 8, seq // 8
@@ -123,30 +128,28 @@
     row = lax.broadcasted_iota(jnp.int32, (ROWS, rows), 0)
     spots = [lane == q * (rows // 2) + j * ROWS + row for q in range(2)]
 
-    def scatter(i, resp, mass):
-        mass_src[i, 0] = mass
-        for h in range(2):
-            w = jnp.dot(resp, x_ref[:, cut[h]], preferred_element_type=F32)
-            w_src[i, h] = w.astype(BF16).reshape(2, rows // 2, width // 2)
-            if i == 0:
-                mine = pl.ds(pl.multiple_of(j * ROWS, ROWS), ROWS)
-                w_src[0, h, hi, mine, :] = (
-                    w_src[0, h, hi, mine, :].astype(F32)
-                    + c_ref[pl.ds(pl.multiple_of(seq * ROWS, ROWS), ROWS), cut[h]]
-                ).astype(BF16)
+    def scatter(i, resp):
+        for h, cut in enumerate(cuts[i]):
+            w = jnp.dot(resp, x_ref[:, cut], preferred_element_type=F32)
+            w_src[i][h] = w.astype(BF16).reshape(2, rows // 2, size[i])
             for k in range(n_oct):
                 theirs = pl.ds(pl.multiple_of(octet_index[k] * ROWS, ROWS), ROWS)
-                send(w_src.at[i, h, :, theirs], w_buf.at[i, h, k], w_s.at[i, h], w_r.at[i, h], octet[k])
-            pending.append(lambda h=h: drain(w_buf.at[i, h], w_s.at[i, h]))
+                send(w_src[i].at[h, :, theirs], w_buf[i].at[h, k], w_s.at[i, h], w_r.at[i, h], octet[k])
+            pending.append(lambda h=h: drain(w_buf[i].at[h], w_s.at[i, h]))
             if h == 0:
+                mass = lax.dot_general(
+                    jnp.ones((16, tokens), BF16), resp, (((1,), (1,)), ((), ())),
+                    preferred_element_type=F32,
+                )
+                mass_src[i, 0] = mass[0:1]
                 for k in range(n_oct):
                     send(mass_src.at[i, 0], mass_buf.at[i, k], m_s.at[i], m_r.at[i], octet[k])
                 pending.append(lambda: drain(mass_buf.at[i], m_s.at[i]))
 
     def partial(i, h, side):
-        acc = w_buf[i, h, 0, side].astype(F32)
+        acc = w_buf[i][h, 0, side].astype(F32)
         for k in range(1, n_oct):
-            acc = acc + w_buf[i, h, k, side].astype(F32)
+            acc = acc + w_buf[i][h, k, side].astype(F32)
         return acc
 
     def pair_up_mass(i):
@@ -157,9 +160,9 @@
         pending.append(lambda: drain(pair_mass.at[i], n_s.at[i]))
         return mass
 
-    scatter(0, *softmax(0, [c0[:, cut[h]].astype(BF16) for h in range(2)], half0))
-    for h in range(2):
-        drain(w_buf.at[0, h], w_r.at[0, h])
+    scatter(0, softmax(0, [c0[:, cut].astype(BF16) for cut in cuts[0]], half0))
+    for h in range(PIECES[0]):
+        drain(w_buf[0].at[h], w_r.at[0, h])
         for q in range(2):
             pair_src[h, q] = partial(0, h, q).astype(BF16)
         send(pair_src.at[h], pair_buf.at[h], o_s.at[h], o_r.at[h], across)
@@ -171,12 +174,13 @@
     bottoms = [jnp.sum(jnp.where(s, mass, 0.0), axis=1, keepdims=True) + 1.0 for s in spots]
     halves = [jnp.zeros((ROWS, 1), F32) for _ in range(2)]
     block = pl.ds(pl.multiple_of(j * ROWS, ROWS), ROWS)
-    for h in range(2):
+    drain(theirs_c, a_r)
+    for h, cut in enumerate(cuts[0]):
         drain(pair_buf.at[h], o_r.at[h])
         for q in range(2):
             both = pair_src[h, q].astype(F32) + pair_buf[h, q].astype(F32)
-            centre = both / bottoms[q]
-            own[q, :, cut[h]] = centre
+            centre = (both + theirs_c[q, :, cut]) / bottoms[q]
+            own[q, :, cut] = centre
             c_src[h, q] = centre.astype(BF16)
             halves[q] += 0.5 * jnp.sum(centre * centre, axis=1, keepdims=True)
         for k in range(n_oct):
@@ -188,8 +192,8 @@
     for k in range(n_oct):
         send(sq_src, sq_buf.at[j], q_s, q_r, octet[k])
     pending.append(lambda: drain(sq_buf, q_s))
-    drain(c_next.at[0], c_r.at[0])
-    drain(c_next.at[1], c_r.at[1])
+    for h in range(PIECES[0]):
+        drain(c_next.at[h], c_r.at[h])
     drain(sq_buf, q_r)
     line = jnp.sum(sq_buf[...], axis=0)
     diagonal = lax.broadcasted_iota(jnp.int32, (rows, rows), 0) == lax.broadcasted_iota(
@@ -197,10 +201,10 @@
     )
     half1 = jnp.sum(jnp.where(diagonal, line, 0.0), axis=1, keepdims=True)
 
-    scatter(1, *softmax(1, [c_next[h].reshape(rows, width // 2) for h in range(2)], half1))
+    scatter(1, softmax(1, [c_next[h].reshape(rows, size[0]) for h in range(PIECES[0])], half1))
     kept = []
-    for h in range(2):
-        drain(w_buf.at[1, h], w_r.at[1, h])
+    for h in range(PIECES[1]):
+        drain(w_buf[1].at[h], w_r.at[1, h])
         last_src[h] = partial(1, h, 1 - hi).astype(BF16)
         send(last_src.at[h], last_buf.at[h], l_s.at[h], l_r.at[h], across)
         pending.append(lambda h=h: drain(last_buf.at[h], l_s.at[h]))
@@ -218,29 +222,26 @@
     near, far = len(NEAR), len(FAR)
     slots = [1 + near + k for k in range(far)] + [1 + k for k in range(near)]
     first, count = (1, 1 + near), (near, far)
-    for h in range(2):
-        fin[1, 0, :, cut[h]] = ((summed(h) + own[hi, :, cut[h]]) / bottom).astype(BF16)
+    for h, cut in enumerate(cuts[1]):
+        fin[1, 0, :, cut] = ((summed(h) + own[hi, :, cut]) / bottom).astype(BF16)
+        lanes = pl.ds(cut.start, size[1])
         for k, slot in enumerate(slots):
             g = 1 if k < far else 0
-            lanes = pl.ds(cut[h].start, width // 2)
             send(fin.at[1, 0, :, lanes], fin.at[0, slot, :, lanes], f_s.at[g, h], f_r.at[g, h], peers_other[k])
-    send(fin.at[1, 0], fin.at[0, 0], p_s.at[0], p_r.at[0], partner)
-    pending.append(lambda: drain(fin.at[0, 0], p_s.at[0]))
-    parts = [
-        [fin.at[0, pl.ds(first[g], count[g]), :, pl.ds(cut[h].start, width // 2)] for h in range(2)]
-        for g in range(2)
-    ]
-    sides = [[fin.at[c, pl.ds(first[g], count[g])] for g in range(2)] for c in range(2)]
+    send(fin.at[1, 0], fin.at[0, 0], p_s, p_r, partner)
+    pending.append(lambda: drain(fin.at[0, 0], p_s))
+
+    def part(c, g, h):
+        return fin.at[c, pl.ds(first[g], count[g]), :, pl.ds(cuts[1][h].start, size[1])]
+
     for g in range(2):
-        for h in range(2):
-            pending.append(lambda g=g, h=h: drain(parts[g][h], f_s.at[g, h]))
-    for g in range(2):
-        for h in range(2):
-            drain(parts[g][h], f_r.at[g, h])
-        send(sides[0][g], sides[1][g], p_s.at[g + 1], p_r.at[g + 1], partner)
-        pending.append(lambda g=g: drain(sides[1][g], p_s.at[g + 1]))
+        for h in range(PIECES[1]):
+            pending.append(lambda g=g, h=h: drain(part(0, g, h), f_s.at[g, h]))
+            drain(part(0, g, h), f_r.at[g, h])
+            send(part(0, g, h), part(1, g, h), h_s.at[g, h], h_r.at[g, h], partner)
+            pending.append(lambda g=g, h=h: drain(part(1, g, h), h_s.at[g, h]))
     pending.pop(0)()
-    drain(fin.at[0, 0], p_r.at[0])
+    drain(fin.at[0, 0], p_r)
     me = lax.axis_index("grp")
     mc, my, mz = me % CORES, (me // CORES) % YS, me // (CORES * YS)
     chips = [(0, 0)] + NEAR + FAR
@@ -254,9 +255,11 @@
             out_ref[g] = d[k * ROWS : (k + 1) * ROWS]
 
     decode(0, 0, 2 * far)
-    drain(sides[1][0], p_r.at[1])
+    for h in range(PIECES[1]):
+        drain(part(1, 0, h), h_r.at[0, h])
     decode(1, 0, far)
-    drain(sides[1][1], p_r.at[2])
+    for h in range(PIECES[1]):
+        drain(part(1, 1, h), h_r.at[1, h])
     decode(1, far, far)
 
     for wait in pending:
@@ -270,6 +273,7 @@
         cols = e.shape[1]
         n_grp = ZH * YS * CORES
         n_oct = len(OCTET) + 1
+        n0, n1 = PIECES
         hbm = pl.BlockSpec(memory_space=pltpu.HBM)
         dma = pltpu.SemaphoreType.DMA
         x, c, e = (pltpu.with_memory_space_constraint(v, pltpu.HBM) for v in (x, c, e))
@@ -283,27 +287,30 @@
                 pltpu.VMEM((rows, width), F32),
                 pltpu.VMEM((width, cols), BF16),
                 pltpu.VMEM((2, ROWS, width), F32),
+                pltpu.VMEM((2, ROWS, width), F32),
                 pltpu.VMEM((2, n_grp - 1, 1, t), F32),
                 pltpu.VMEM((2, 1, t), F32),
                 pltpu.VMEM((2, n_oct, 1, rows), F32),
                 pltpu.VMEM((2, 2, 1, rows), F32),
                 pltpu.VMEM((2, 1, rows), F32),
-                pltpu.VMEM((2, 2, 2, rows // 2, width // 2), BF16),
-                pltpu.VMEM((2, 2, n_oct, 2, ROWS, width // 2), BF16),
-                pltpu.VMEM((2, 2, ROWS, width // 2), BF16),
-                pltpu.VMEM((2, 2, ROWS, width // 2), BF16),
-                pltpu.VMEM((2, ROWS, width // 2), BF16),
-                pltpu.VMEM((2, ROWS, width // 2), BF16),
-                pltpu.VMEM((2, 2, ROWS, width // 2), BF16),
-                pltpu.VMEM((2, 2, rows // 2, width // 2), BF16),
+                pltpu.VMEM((n0, 2, rows // 2, width // n0), BF16),
+                pltpu.VMEM((n1, 2, rows // 2, width // n1), BF16),
+                pltpu.VMEM((n0, n_oct, 2, ROWS, width // n0), BF16),
+                pltpu.VMEM((n1, n_oct, 2, ROWS, width // n1), BF16),
+                pltpu.VMEM((n0, 2, ROWS, width // n0), BF16),
+                pltpu.VMEM((n0, 2, ROWS, width // n0), BF16),
+                pltpu.VMEM((n1, ROWS, width // n1), BF16),
+                pltpu.VMEM((n1, ROWS, width // n1), BF16),
+                pltpu.VMEM((n0, 2, ROWS, width // n0), BF16),
+                pltpu.VMEM((n0, 2, rows // 2, width // n0), BF16),
                 pltpu.VMEM((1, rows), F32),
                 pltpu.VMEM((n_oct, 1, rows), F32),
                 pltpu.VMEM((2, n_grp // 2, ROWS, width), BF16),
-                dma, dma, dma,
+                dma, dma, dma, dma, dma,
                 dma((2,)), dma((2,)), dma((2,)), dma((2,)), dma((2,)), dma((2,)),
-                dma((2, 2)), dma((2, 2)), dma((2,)), dma((2,)), dma((2,)), dma((2,)),
-                dma((2,)), dma((2,)), dma, dma,
-                dma((2, 2)), dma((2, 2)), dma((3,)), dma((3,)),
+                dma((2, max(PIECES))), dma((2, max(PIECES))), dma((n0,)), dma((n0,)), dma((n1,)), dma((n1,)),
+                dma((n0,)), dma((n0,)), dma, dma,
+                dma((2, n1)), dma((2, n1)), dma, dma, dma((2, n1)), dma((2, n1)),
             ],
             compiler_params=pltpu.CompilerParams(
                 collective_id=0, has_side_effects=True, vmem_limit_bytes=24 * 2**20

time: 64.9 us -> 64.7 us (level)
  no operation moved by 1% of the time
where the time goes in v7:
time: 64.7 us; the launch traced here: 64.5 us
  Pallas kernels  62.9 us (97%)
  local copies, waits for them, and re-layouts  0.97 us (1%)
  between operations  0.66 us (1%)
    pallas_call x1, Pallas kernels, per_device(): pl.pallas_call(kernel, out_shape=jax.ShapeDtypeStruct((n_grp, ROWS, cols)...  62.9 us

profile of v7, /device:TPU:1, one launch (start us, length us, event | category | flops | bytes accessed | tf_op | source)
XLA Modules:
  0.0 64.5 jit_solution(8089183291939332500)
XLA Ops:
  0.7 62.9 %kmeans_decode.1 = bf16[32,16,1024]{2,1,0:T(8,128)(2,1)S(1)} custom-call(bf16[512,512]{1,0:T(8,128)(2,1)} %x_hbm.1, f32[256,512]{1,0:T(8,128)} %c_hbm.1, f32[1]{0:T(128)S(6)} %copy.6.scale_ref, bf16[512,1024]{1,0:T(8,128)(2,1)} %e_hbm.1), custom_call_target="tpu_custom_call" | custom-call | tf_op jit(solution)/shard_map/kmeans_decode/pallas_call | solution.py:280
  63.5 1.0 %copy.7 = bf16[32,16,1024]{2,1,0:T(8,128)(2,1)} copy(bf16[32,16,1024]{2,1,0:T(8,128)(2,1)S(1)} %kmeans_decode.1) | data formatting | bytes 2097152

commit v8 on v7

--- a/solution.py
+++ b/solution.py
@@ -42,9 +42,9 @@
 
 def kernel(
     x_hbm, c_hbm, scale_ref, e_hbm, out_ref,
-    x_ref, c_ref, e_ref, own, theirs_c, lse_buf, lse_src, mass_buf, mass_src, pair_mass,
+    x_ref, c_ref, e_ref, own, theirs_c, lse_near, lse_half, lse_buf, lse_src, mass_buf, mass_src, pair_mass,
     w_src0, w_src1, w_buf0, w_buf1, pair_src, pair_buf, last_src, last_buf, c_src, c_next, sq_src, sq_buf, fin,
-    x_sem, c_sem, e_sem, a_s, a_r,
+    x_sem, c_sem, e_sem, a_s, a_r, b_s, b_r,
     lse_s, lse_r, m_s, m_r, n_s, n_r, w_s, w_r, o_s, o_r, l_s, l_r,
     c_s, c_r, q_s, q_r, f_s, f_r, p_s, p_r, h_s, h_r,
 ):
@@ -59,15 +59,17 @@
     peers_chip = [{"grp": grp_index(z, y, 0)} for z, y in CHIPS]
     peers_other = [{"grp": grp_index(z, y, 1)} for z, y in CHIPS]
     partner = {"grp": partner_group}
-    everyone = [p for pair in zip(peers_chip, peers_other) for p in pair] + octet + [across]
-
+    near_both = [p for pair in zip(peers_chip[len(FAR) :], peers_other[len(FAR) :]) for p in pair] + [partner]
+    opposite = {"grp": grp_index(1, 0, 1)}
+    everyone = [opposite] + near_both + octet[:-1] + [across]
+
+    barrier = pltpu.get_barrier_semaphore()
+    for p in everyone:
+        pl.semaphore_signal(barrier, inc=1, device_id=p, device_id_type=MESH)
     c_copy = pltpu.make_async_copy(c_hbm, c_ref, c_sem)
     c_copy.start()
     x_copy = pltpu.make_async_copy(x_hbm, x_ref, x_sem)
     x_copy.start()
-    barrier = pltpu.get_barrier_semaphore()
-    for p in everyone:
-        pl.semaphore_signal(barrier, inc=1, device_id=p, device_id_type=MESH)
     e_copy = pltpu.make_async_copy(e_hbm, e_ref, e_sem)
     e_copy.start()
     pending = [e_copy.wait]
@@ -88,6 +90,10 @@
     x_copy.wait()
     size = [width // n for n in PIECES]
     cuts = [[slice(h * size[i], (h + 1) * size[i]) for h in range(n)] for i, n in enumerate(PIECES)]
+
+    def merge(others, lse):
+        m = jnp.maximum(jnp.max(others, axis=0), lse)
+        return m + jnp.log(jnp.sum(jnp.exp(others - m[None]), axis=0) + jnp.exp(lse - m))
 
     def softmax(i, centres, half):
         dots = sum(
@@ -102,23 +108,31 @@
         lse_src[i] = lse
         if i == 0:
             pl.semaphore_wait(barrier, len(everyone))
-        slot = 0
-        for a, b in zip(peers_chip, peers_other):
-            for p in (a, b):
-                send(lse_src.at[i], lse_buf.at[i, slot], lse_s.at[i], lse_r.at[i], p)
-                slot += 1
-        send(lse_src.at[i], lse_buf.at[i, slot], lse_s.at[i], lse_r.at[i], partner)
-        pending.append(lambda: drain(lse_buf.at[i], lse_s.at[i]))
         if i == 0:
+            for slot, p in enumerate(near_both):
+                send(lse_src.at[0], lse_near.at[slot], lse_s.at[0], lse_r.at[0], p)
             for q in range(2):
                 start = pl.ds(pl.multiple_of(q * (rows // 2) + (seq % 8) * ROWS, ROWS), ROWS)
                 send(c_ref.at[start], theirs_c.at[q], a_s, a_r, partner)
+            pending.append(lambda: drain(lse_near, lse_s.at[0]))
             pending.append(lambda: drain(theirs_c, a_s))
-        drain(lse_buf.at[i], lse_r.at[i])
-        others = lse_buf[i]
-        m = jnp.maximum(jnp.max(others, axis=0), lse)
-        total = jnp.sum(jnp.exp(others - m[None]), axis=0) + jnp.exp(lse - m)
-        full = m + jnp.log(total)
+            drain(lse_near, lse_r.at[0])
+            near = merge(lse_near[...], lse)
+            lse_half[0] = near
+            send(lse_half.at[0], lse_half.at[1], b_s, b_r, opposite)
+            pending.append(lambda: drain(lse_half.at[1], b_s))
+            drain(lse_half.at[1], b_r)
+            full = merge(lse_half[1:2], near)
+        else:
+            slot = 0
+            for a, b in zip(peers_chip, peers_other):
+                for p in (a, b):
+                    send(lse_src.at[1], lse_buf.at[slot], lse_s.at[1], lse_r.at[1], p)
+                    slot += 1
+            send(lse_src.at[1], lse_buf.at[slot], lse_s.at[1], lse_r.at[1], partner)
+            pending.append(lambda: drain(lse_buf, lse_s.at[1]))
+            drain(lse_buf, lse_r.at[1])
+            full = merge(lse_buf[...], lse)
         resp = jnp.exp(logits - full).astype(BF16)
         return resp
 
@@ -288,7 +302,9 @@
                 pltpu.VMEM((width, cols), BF16),
                 pltpu.VMEM((2, ROWS, width), F32),
                 pltpu.VMEM((2, ROWS, width), F32),
-                pltpu.VMEM((2, n_grp - 1, 1, t), F32),
+                pltpu.VMEM((n_grp // 2 - 1, 1, t), F32),
+                pltpu.VMEM((2, 1, t), F32),
+                pltpu.VMEM((n_grp - 1, 1, t), F32),
                 pltpu.VMEM((2, 1, t), F32),
                 pltpu.VMEM((2, n_oct, 1, rows), F32),
                 pltpu.VMEM((2, 2, 1, rows), F32),
@@ -306,7 +322,7 @@
                 pltpu.VMEM((1, rows), F32),
                 pltpu.VMEM((n_oct, 1, rows), F32),
                 pltpu.VMEM((2, n_grp // 2, ROWS, width), BF16),
-                dma, dma, dma, dma, dma,
+                dma, dma, dma, dma, dma, dma, dma,
                 dma((2,)), dma((2,)), dma((2,)), dma((2,)), dma((2,)), dma((2,)),
                 dma((2, max(PIECES))), dma((2, max(PIECES))), dma((n0,)), dma((n0,)), dma((n1,)), dma((n1,)),
                 dma((n0,)), dma((n0,)), dma, dma,

time: 64.7 us -> 65.5 us (1.012)
  Pallas kernels: 62.9 us -> 63.7 us
    pallas_call x1, Pallas kernels: 62.9 us -> 63.7 us  [per_device(): pl.pallas_call(kernel, out_shape=jax.ShapeDtypeStruct((n_grp, ROWS, cols)...]
where the time goes in v8:
time: 65.5 us; the launch traced here: 65.3 us
  Pallas kernels  63.7 us (97%)
  local copies, waits for them, and re-layouts  0.97 us (1%)
  between operations  0.66 us (1%)
    pallas_call x1, Pallas kernels, per_device(): pl.pallas_call(kernel, out_shape=jax.ShapeDtypeStruct((n_grp, ROWS, cols)...  63.7 us

profile of v8, /device:TPU:1, one launch (start us, length us, event | category | flops | bytes accessed | tf_op | source)
XLA Modules:
  0.0 65.3 jit_solution(18245361071515773059)
XLA Ops:
  0.7 63.7 %kmeans_decode.1 = bf16[32,16,1024]{2,1,0:T(8,128)(2,1)S(1)} custom-call(bf16[512,512]{1,0:T(8,128)(2,1)} %x_hbm.1, f32[256,512]{1,0:T(8,128)} %c_hbm.1, f32[1]{0:T(128)S(6)} %copy.6.scale_ref, bf16[512,1024]{1,0:T(8,128)(2,1)} %e_hbm.1), custom_call_target="tpu_custom_call" | custom-call | tf_op jit(solution)/shard_map/kmeans_decode/pallas_call | solution.py:294
  64.3 1.0 %copy.7 = bf16[32,16,1024]{2,1,0:T(8,128)(2,1)} copy(bf16[32,16,1024]{2,1,0:T(8,128)(2,1)S(1)} %kmeans_decode.1) | data formatting | bytes 2097152

commit v9 on v7

--- a/solution.py
+++ b/solution.py
@@ -61,13 +61,13 @@
     partner = {"grp": partner_group}
     everyone = [p for pair in zip(peers_chip, peers_other) for p in pair] + octet + [across]
 
+    barrier = pltpu.get_barrier_semaphore()
+    for p in everyone:
+        pl.semaphore_signal(barrier, inc=1, device_id=p, device_id_type=MESH)
     c_copy = pltpu.make_async_copy(c_hbm, c_ref, c_sem)
     c_copy.start()
     x_copy = pltpu.make_async_copy(x_hbm, x_ref, x_sem)
     x_copy.start()
-    barrier = pltpu.get_barrier_semaphore()
-    for p in everyone:
-        pl.semaphore_signal(barrier, inc=1, device_id=p, device_id_type=MESH)
     e_copy = pltpu.make_async_copy(e_hbm, e_ref, e_sem)
     e_copy.start()
     pending = [e_copy.wait]
@@ -98,7 +98,8 @@
         )
         logits = factor * (dots - half)
         top = jnp.max(logits, axis=0, keepdims=True)
-        lse = top + jnp.log(jnp.sum(jnp.exp(logits - top), axis=0, keepdims=True))
+        weights = jnp.exp(logits - top)
+        lse = top + jnp.log(jnp.sum(weights, axis=0, keepdims=True))
         lse_src[i] = lse
         if i == 0:
             pl.semaphore_wait(barrier, len(everyone))
@@ -119,7 +120,7 @@
         m = jnp.maximum(jnp.max(others, axis=0), lse)
         total = jnp.sum(jnp.exp(others - m[None]), axis=0) + jnp.exp(lse - m)
         full = m + jnp.log(total)
-        resp = jnp.exp(logits - full).astype(BF16)
+        resp = (weights * jnp.exp(top - full)).astype(BF16)
         return resp
 
     n_oct = len(octet)
@@ -246,21 +247,28 @@
     mc, my, mz = me % CORES, (me // CORES) % YS, me // (CORES * YS)
     chips = [(0, 0)] + NEAR + FAR
 
-    def decode(half, first, count):
-        part = fin[half, first : first + count].reshape(count * ROWS, width)
-        d = jnp.dot(part, e_ref[...], preferred_element_type=F32).astype(BF16)
+    def place(half, first, count, d):
         for k in range(count):
             z, y = chips[first + k]
             g = (((mz + ZH - z) % ZH) * YS + (my + YS - y) % YS) * CORES + (mc + half) % CORES
             out_ref[g] = d[k * ROWS : (k + 1) * ROWS]
 
+    def decode(half, first, count):
+        part = fin[half, first : first + count].reshape(count * ROWS, width)
+        d = jnp.dot(part, e_ref[...], preferred_element_type=F32).astype(BF16)
+        place(half, first, count, d)
+
     decode(0, 0, 2 * far)
     for h in range(PIECES[1]):
         drain(part(1, 0, h), h_r.at[0, h])
     decode(1, 0, far)
-    for h in range(PIECES[1]):
+    d = None
+    for h, cut in enumerate(cuts[1]):
         drain(part(1, 1, h), h_r.at[1, h])
-    decode(1, far, far)
+        rows_h = fin[1, far : 2 * far, :, cut].reshape(far * ROWS, size[1])
+        d_h = jnp.dot(rows_h, e_ref[cut, :], preferred_element_type=F32)
+        d = d_h if d is None else d + d_h
+    place(1, far, far, d.astype(BF16))
 
     for wait in pending:
         wait()

time: 64.7 us -> 65.1 us (level)
  no operation moved by 1% of the time
where the time goes in v9:
time: 65.1 us; the launch traced here: 64.9 us
  Pallas kernels  63.3 us (97%)
  local copies, waits for them, and re-layouts  0.97 us (1%)
  between operations  0.66 us (1%)
    pallas_call x1, Pallas kernels, per_device(): pl.pallas_call(kernel, out_shape=jax.ShapeDtypeStruct((n_grp, ROWS, cols)...  63.3 us

profile of v9, /device:TPU:1, one launch (start us, length us, event | category | flops | bytes accessed | tf_op | source)
XLA Modules:
  0.0 64.9 jit_solution(11956796695084644289)
XLA Ops:
  0.7 63.3 %kmeans_decode.1 = bf16[32,16,1024]{2,1,0:T(8,128)(2,1)S(1)} custom-call(bf16[512,512]{1,0:T(8,128)(2,1)} %x_hbm.1, f32[256,512]{1,0:T(8,128)} %c_hbm.1, f32[1]{0:T(128)S(6)} %copy.6.scale_ref, bf16[512,1024]{1,0:T(8,128)(2,1)} %e_hbm.1), custom_call_target="tpu_custom_call" | custom-call | tf_op jit(solution)/shard_map/kmeans_decode/pallas_call | solution.py:288
  63.9 1.0 %copy.7 = bf16[32,16,1024]{2,1,0:T(8,128)(2,1)} copy(bf16[32,16,1024]{2,1,0:T(8,128)(2,1)S(1)} %kmeans_decode.1) | data formatting | bytes 2097152

commit v10 on v7

--- a/solution.py
+++ b/solution.py
@@ -12,7 +12,7 @@
 ZH, YS, CORES = 2, 8, 2
 ROWS = 16
 F32, BF16 = jnp.float32, jnp.bfloat16
-PIECES = (2, 2)
+PIECES = (4, 2)
 
 
 def ring(d, n):

time: 64.7 us -> 64.5 us (level)
  no operation moved by 1% of the time
where the time goes in v10:
time: 64.5 us; the launch traced here: 64.4 us
  Pallas kernels  62.7 us (97%)
  local copies, waits for them, and re-layouts  0.97 us (2%)
  between operations  0.66 us (1%)
    pallas_call x1, Pallas kernels, per_device(): pl.pallas_call(kernel, out_shape=jax.ShapeDtypeStruct((n_grp, ROWS, cols)...  62.7 us

profile of v10, /device:TPU:1, one launch (start us, length us, event | category | flops | bytes accessed | tf_op | source)
XLA Modules:
  0.0 64.4 jit_solution(497812792187867973)
XLA Ops:
  0.7 62.7 %kmeans_decode.1 = bf16[32,16,1024]{2,1,0:T(8,128)(2,1)S(1)} custom-call(bf16[512,512]{1,0:T(8,128)(2,1)} %x_hbm.1, f32[256,512]{1,0:T(8,128)} %c_hbm.1, f32[1]{0:T(128)S(6)} %copy.6.scale_ref, bf16[512,1024]{1,0:T(8,128)(2,1)} %e_hbm.1), custom_call_target="tpu_custom_call" | custom-call | tf_op jit(solution)/shard_map/kmeans_decode/pallas_call | solution.py:280
  63.4 1.0 %copy.7 = bf16[32,16,1024]{2,1,0:T(8,128)(2,1)} copy(bf16[32,16,1024]{2,1,0:T(8,128)(2,1)S(1)} %kmeans_decode.1) | data formatting | bytes 2097152

commit v11 on v9

--- a/solution.py
+++ b/solution.py
@@ -12,7 +12,7 @@
 ZH, YS, CORES = 2, 8, 2
 ROWS = 16
 F32, BF16 = jnp.float32, jnp.bfloat16
-PIECES = (2, 2)
+PIECES = (4, 2)
 
 
 def ring(d, n):

time: 65.1 us -> 64.5 us (level)
  no operation moved by 1% of the time
where the time goes in v11:
time: 64.5 us; the launch traced here: 64.4 us
  Pallas kernels  62.7 us (97%)
  local copies, waits for them, and re-layouts  0.97 us (2%)
  between operations  0.66 us (1%)
    pallas_call x1, Pallas kernels, per_device(): pl.pallas_call(kernel, out_shape=jax.ShapeDtypeStruct((n_grp, ROWS, cols)...  62.7 us

profile of v11, /device:TPU:1, one launch (start us, length us, event | category | flops | bytes accessed | tf_op | source)
XLA Modules:
  0.0 64.4 jit_solution(6497225685793188124)
XLA Ops:
  0.7 62.7 %kmeans_decode.1 = bf16[32,16,1024]{2,1,0:T(8,128)(2,1)S(1)} custom-call(bf16[512,512]{1,0:T(8,128)(2,1)} %x_hbm.1, f32[256,512]{1,0:T(8,128)} %c_hbm.1, f32[1]{0:T(128)S(6)} %copy.6.scale_ref, bf16[512,1024]{1,0:T(8,128)(2,1)} %e_hbm.1), custom_call_target="tpu_custom_call" | custom-call | tf_op jit(solution)/shard_map/kmeans_decode/pallas_call | solution.py:288
  63.4 1.0 %copy.7 = bf16[32,16,1024]{2,1,0:T(8,128)(2,1)} copy(bf16[32,16,1024]{2,1,0:T(8,128)(2,1)S(1)} %kmeans_decode.1) | data formatting | bytes 2097152
